TPU v7x, 256 devices: a whole 4x4x8 slice. The times are simulated.
256 devices in a mesh: mem: 8 (over y, x_hi), space: 32 (over x_lo, z, core).
Axes of the slice: x: 4 (x_hi: 2, x_lo: 2; x = x_hi * 2 + x_lo), y: 4, z: 8, core: 2. Of those that a mesh axis runs over, the one named last changes fastest.
Arguments:
- ens_pert: bfloat16 [80, 127, 65536], P('mem', None, 'space'), may hold values from -6 to 6
- vert_modes: bfloat16 [127, 40], replicated, may hold values from -0.5 to 0.5
- loc_stencil: bfloat16 [1152, 65536], P(None, 'space'), may hold values from -0.1875 to 0.1875
- grad_hi: float32 [127, 262144], P(None, ('mem', 'space')), may hold values from -6 to 6
- child_map: int32 [4, 65536], P(None, 'space'), may hold values from 0 to 8191, as said below
- halo_rows: int32 [2, 32], P(None, 'space'), may hold values from 256 to 512
Outputs:
- control_grad: float32 [80, 40, 65536], P('mem', None, 'space')
Inputs may be any that keep to these rules, and one draw needn't show every extreme that they name: `child_map`: within the 2048 cells of each block, the 8192 codes are each value of the range exactly once.
All inputs are finite; a program needn't handle non-finite values.
Results may differ from a plain program's by a relative error of at most 0.0065.
Values may be sent and summed in bfloat16 or wider, within the bound.
A program may use at most 128 MiB of HBM per device.

v0:
```python
import jax
import jax.numpy as jnp
from jax import lax
from jax.sharding import PartitionSpec as P

TILE = 128
HALO = 512


def padded(block, sides, width):
    for axis, dim in sides:
        count = lax.axis_size(axis)
        forward = [(i, i + 1) for i in range(count - 1)]
        forward.append((count - 1, 0))
        backward = [(target, source) for source, target in forward]
        low = lax.ppermute(
            lax.slice_in_dim(block, block.shape[dim] - width, None, axis=dim), axis, forward
        )
        high = lax.ppermute(lax.slice_in_dim(block, 0, width, axis=dim), axis, backward)
        block = jnp.concatenate([low, block, high], axis=dim)
    return block


def split_parts(values):
    upper = values.astype(jnp.bfloat16)
    lower = (values - upper.astype(jnp.float32)).astype(jnp.bfloat16)
    return (upper, lower)


def smooth(extended, loc_stencil, cell_count):
    tile_count = cell_count // TILE

    def one_tile(first_col):
        window = lax.dynamic_slice_in_dim(extended, first_col, TILE + 2 * HALO, 1)
        weights = lax.dynamic_slice_in_dim(loc_stencil, first_col, TILE, 1)
        return jnp.dot(window, weights, preferred_element_type=jnp.float32)

    tile_results = lax.map(one_tile, jnp.arange(tile_count, dtype=jnp.int32) * TILE)
    return tile_results.transpose(1, 0, 2).reshape(extended.shape[0], cell_count)


def local(ens_pert, vert_modes, loc_stencil, grad_hi, child_map, halo_rows):
    level_count, hi_dev = grad_hi.shape
    members = ens_pert.shape[0]
    cell_count = ens_pert.shape[2]
    relayed = lax.all_to_all(grad_hi, "space", split_axis=1, concat_axis=1, tiled=True)
    gathered = lax.all_gather(relayed, "mem", axis=1, tiled=True)
    picked = jnp.take(gathered, child_map.reshape(-1), axis=1).reshape(level_count, 4, cell_count)
    coarse = 0.25 * jnp.sum(picked, axis=1)
    products = (ens_pert.astype(jnp.float32) * coarse[None]).astype(jnp.bfloat16)
    positions = jnp.arange(cell_count + 2 * HALO, dtype=jnp.int32)
    kept_cols = (positions >= HALO - halo_rows[0, 0]) & (
        positions < HALO + cell_count + halo_rows[1, 0]
    )
    extended = padded(products.reshape(members * level_count, cell_count), (("space", 1),), HALO)
    extended = jnp.where(kept_cols[None, :], extended, jnp.zeros((), jnp.bfloat16))
    smoothed = smooth(extended, loc_stencil, cell_count).reshape(members, level_count, cell_count)
    upper, lower = split_parts(smoothed)
    control_grad = jnp.einsum(
        "lm,klc->kmc", vert_modes, upper, preferred_element_type=jnp.float32
    ) + jnp.einsum("lm,klc->kmc", vert_modes, lower, preferred_element_type=jnp.float32)
    return control_grad


def solution(mesh):
    placed = (
        P("mem", None, "space"),
        P(),
        P(None, "space"),
        P(None, ("mem", "space")),
        P(None, "space"),
        P(None, "space"),
    )
    return jax.shard_map(
        local, mesh=mesh, in_specs=placed, out_specs=P("mem", None, "space"), check_vma=False
    )
```

profile of v0, /device:TPU:1, one launch (start us, length us, event | category | flops | bytes accessed | tf_op | source)
XLA Modules:
  0.0 357.0 jit_solution(526599996994217665)
XLA Ops:
  6.5 0.0 copy-start
  6.5 0.0 all-gather.2.cloned.1.call-start
  6.5 1.3 copy.10
  7.8 27.5 %all_to_all.12 = f32[127,32,32]{0,2,1:T(8,128)} all-to-all(f32[127,32,32]{0,2,1:T(8,128)S(1)} %bitcast.32), channel_id=1, replica_groups=mesh['mem'=8,'space'=32] {'space'}, dimensions={1} | all-to-all | bytes 1040384 | tf_op jit(solution)/shard_map/all_to_all | solution.py:46
  35.3 0.0 all-gather.2.cloned.1.call-update
  35.4 0.8 copy.13
  36.2 0.8 compare_and_fusion
  37.0 72.6 %all-gather.2.cloned.1.call-done = f32[127,8192]{0,1:T(8,128)} async-done(((f32[127,1024]{0,1:T(8,128)}), f32[127,8192]{0,1:T(8,128)}) %all-gather.2.cloned.1.call-update) | async-done | bytes 4161552 | tf_op jit(solution)/shard_map/all_gather | solution.py:47
  109.6 30.1 %gather_fusion = f32[8192,127]{1,0:T(8,128)} fusion(f32[127,8192]{0,1:T(8,128)} %all-gather.2.cloned.1.call-done, s32[8192]{0:T(1024)S(1)} %broadcast_clamp_fusion), kind=kCustom, calls=%fused_computation | custom fusion | bytes 8355840 | tf_op jit(solution)/shard_map/jit(_take)/gather | solution.py:48
  139.7 3.7 %select_reduce_fusion = f32[127,2048]{0,1:T(8,128)S(1)} fusion(f32[127,4,2048]{0,2,1:T(8,128)} %bitcast.29, pred[4,2048]{1,0:T(4,128)(4,1)S(1)} %compare_and_fusion), kind=kLoop, calls=%fused_computation.11 | loop fusion | flops 1820672 | bytes 5210112 | tf_op jit(solution)/shard_map/reduce_sum | solution.py:49
  143.4 0.1 broadcast_multiply_fusion
  143.4 0.4 copy.11
  143.8 6.6 %multiply_convert_fusion = bf16[10,127,2048]{2,1,0:T(8,128)(2,1)} fusion(bf16[10,127,2048]{2,1,0:T(8,128)(2,1)} %param.8, f32[127,2048]{1,0:T(8,128)S(1)} %copy.11), kind=kLoop, calls=%fused_computation.8 | loop fusion | flops 7802880 | bytes 11444224 | tf_op jit(solution)/shard_map/convert_element_type | solution.py:50
  150.4 0.0 copy-start.2
  150.4 5.7 %reshape.63 = bf16[1270,2048]{1,0:T(8,128)(2,1)} reshape(bf16[10,127,2048]{2,1,0:T(8,128)(2,1)} %multiply_convert_fusion) | data formatting | bytes 10403840 | tf_op jit(solution)/shard_map/reshape | solution.py:55
  156.2 1.9 fusion.16
  158.1 2.3 collective-permute-start
  160.4 0.0 collective-permute-start.1
  160.4 0.0 copy-done.2
  160.4 0.6 fusion.17
  162.1 12.7 %collective-permute-done = bf16[1270,512]{1,0:T(8,128)(2,1)} collective-permute-done((bf16[1270,512]{1,0:T(8,128)(2,1)S(1)}, bf16[1270,512]{1,0:T(8,128)(2,1)}, u32[]{:S(2)}, u32[]{:S(2)}) %collective-permute-start) | collective-permute-done | bytes 1300512 | tf_op jit(solution)/shard_map/ppermute | solution.py:16
  174.8 2.9 collective-permute-done.1
  177.7 7.5 %maximum_select_fusion = bf16[1270,3072]{1,0:T(8,128)(2,1)} fusion(bf16[1270,512]{1,0:T(8,128)(2,1)} %collective-permute-done.1, bf16[1270,2048]{1,0:T(8,128)(2,1)} %reshape.63, bf16[1270,512]{1,0:T(8,128)(2,1)} %collective-permute-done, pred[3072]{0:T(1024)(128)(4,1)S(1)} %fusion.13), kind=kLoop, calls=%fused_computation.9 | loop fusion | flops 27310080 | bytes 15608832 | tf_op jit(solution)/shard_map/jit(_where)/select_n | solution.py:56
  185.2 129.8 %while.10 = (s32[]{:T(128)}, f32[16,1270,128]{2,1,0:T(8,128)}, s32[16]{0:T(128)S(1)}, bf16[1270,3072]{1,0:T(8,128)(2,1)}, bf16[1152,2048]{1,0:T(8,128)(2,1)}, /*index=5*/s32[]{:T(128)}, s32[]{:T(128)}, s32[]{:T(128)}, s32[]{:T(128)}) while((s32[]{:T(128)}, f32[16,1270,128]{2,1,0:T(8,128)}, s32[16]{0:T(128)S(1)}, bf16[1270,3072]{1,0:T(8,128)(2,1)}, ...), condition=%wide.region_2.3_spmd, body=%wide.region_1.2_spmd.sunk | while | flops 374538240 | bytes 3877548 | solution.py:38
  185.2 0.6 dynamic_slice.23
  189.0 4.3 %fusion.23 = f32[16,1270,128]{2,1,0:T(8,128)} fusion(f32[16,1270,128]{2,1,0:T(8,128)} %get-tuple-element.88, s32[]{:T(128)} %get-tuple-element.87, bf16[1270,3072]{1,0:T(8,128)(2,1)} %get-tuple-element.99, s32[]{:T(128)S(6)} %select_n.44, bf16[1152,2048]{1,0:T(8,128)(2,1)} %get-tuple-element.100, s32[]{:T(128)S(6)} %select_n.45), kind=kOutput, calls=%fused_computation.4.clone.1 | convolution fusion | flops 374538240 | bytes 3877384 | tf_op jit(solution)/shard_map/while/body/eval_jaxpr/dot_general | solution.py:36
  193.3 0.6 dynamic_slice.23
  197.1 4.3 %fusion.23 = f32[16,1270,128]{2,1,0:T(8,128)} fusion(f32[16,1270,128]{2,1,0:T(8,128)} %get-tuple-element.88, s32[]{:T(128)} %get-tuple-element.87, bf16[1270,3072]{1,0:T(8,128)(2,1)} %get-tuple-element.99, s32[]{:T(128)S(6)} %select_n.44, bf16[1152,2048]{1,0:T(8,128)(2,1)} %get-tuple-element.100, s32[]{:T(128)S(6)} %select_n.45), kind=kOutput, calls=%fused_computation.4.clone.1 | convolution fusion | flops 374538240 | bytes 3877384 | tf_op jit(solution)/shard_map/while/body/eval_jaxpr/dot_general | solution.py:36
  201.4 0.6 dynamic_slice.23
  205.2 4.4 %fusion.23 = f32[16,1270,128]{2,1,0:T(8,128)} fusion(f32[16,1270,128]{2,1,0:T(8,128)} %get-tuple-element.88, s32[]{:T(128)} %get-tuple-element.87, bf16[1270,3072]{1,0:T(8,128)(2,1)} %get-tuple-element.99, s32[]{:T(128)S(6)} %select_n.44, bf16[1152,2048]{1,0:T(8,128)(2,1)} %get-tuple-element.100, s32[]{:T(128)S(6)} %select_n.45), kind=kOutput, calls=%fused_computation.4.clone.1 | convolution fusion | flops 374538240 | bytes 3877384 | tf_op jit(solution)/shard_map/while/body/eval_jaxpr/dot_general | solution.py:36
  209.6 0.6 dynamic_slice.23
  213.3 4.3 %fusion.23 = f32[16,1270,128]{2,1,0:T(8,128)} fusion(f32[16,1270,128]{2,1,0:T(8,128)} %get-tuple-element.88, s32[]{:T(128)} %get-tuple-element.87, bf16[1270,3072]{1,0:T(8,128)(2,1)} %get-tuple-element.99, s32[]{:T(128)S(6)} %select_n.44, bf16[1152,2048]{1,0:T(8,128)(2,1)} %get-tuple-element.100, s32[]{:T(128)S(6)} %select_n.45), kind=kOutput, calls=%fused_computation.4.clone.1 | convolution fusion | flops 374538240 | bytes 3877384 | tf_op jit(solution)/shard_map/while/body/eval_jaxpr/dot_general | solution.py:36
  217.7 0.6 dynamic_slice.23
  221.4 4.3 %fusion.23 = f32[16,1270,128]{2,1,0:T(8,128)} fusion(f32[16,1270,128]{2,1,0:T(8,128)} %get-tuple-element.88, s32[]{:T(128)} %get-tuple-element.87, bf16[1270,3072]{1,0:T(8,128)(2,1)} %get-tuple-element.99, s32[]{:T(128)S(6)} %select_n.44, bf16[1152,2048]{1,0:T(8,128)(2,1)} %get-tuple-element.100, s32[]{:T(128)S(6)} %select_n.45), kind=kOutput, calls=%fused_computation.4.clone.1 | convolution fusion | flops 374538240 | bytes 3877384 | tf_op jit(solution)/shard_map/while/body/eval_jaxpr/dot_general | solution.py:36
  225.8 0.6 dynamic_slice.23
  229.5 4.3 %fusion.23 = f32[16,1270,128]{2,1,0:T(8,128)} fusion(f32[16,1270,128]{2,1,0:T(8,128)} %get-tuple-element.88, s32[]{:T(128)} %get-tuple-element.87, bf16[1270,3072]{1,0:T(8,128)(2,1)} %get-tuple-element.99, s32[]{:T(128)S(6)} %select_n.44, bf16[1152,2048]{1,0:T(8,128)(2,1)} %get-tuple-element.100, s32[]{:T(128)S(6)} %select_n.45), kind=kOutput, calls=%fused_computation.4.clone.1 | convolution fusion | flops 374538240 | bytes 3877384 | tf_op jit(solution)/shard_map/while/body/eval_jaxpr/dot_general | solution.py:36
  233.9 0.6 dynamic_slice.23
  237.6 4.4 %fusion.23 = f32[16,1270,128]{2,1,0:T(8,128)} fusion(f32[16,1270,128]{2,1,0:T(8,128)} %get-tuple-element.88, s32[]{:T(128)} %get-tuple-element.87, bf16[1270,3072]{1,0:T(8,128)(2,1)} %get-tuple-element.99, s32[]{:T(128)S(6)} %select_n.44, bf16[1152,2048]{1,0:T(8,128)(2,1)} %get-tuple-element.100, s32[]{:T(128)S(6)} %select_n.45), kind=kOutput, calls=%fused_computation.4.clone.1 | convolution fusion | flops 374538240 | bytes 3877384 | tf_op jit(solution)/shard_map/while/body/eval_jaxpr/dot_general | solution.py:36
  242.1 0.6 dynamic_slice.23
  245.8 4.3 %fusion.23 = f32[16,1270,128]{2,1,0:T(8,128)} fusion(f32[16,1270,128]{2,1,0:T(8,128)} %get-tuple-element.88, s32[]{:T(128)} %get-tuple-element.87, bf16[1270,3072]{1,0:T(8,128)(2,1)} %get-tuple-element.99, s32[]{:T(128)S(6)} %select_n.44, bf16[1152,2048]{1,0:T(8,128)(2,1)} %get-tuple-element.100, s32[]{:T(128)S(6)} %select_n.45), kind=kOutput, calls=%fused_computation.4.clone.1 | convolution fusion | flops 374538240 | bytes 3877384 | tf_op jit(solution)/shard_map/while/body/eval_jaxpr/dot_general | solution.py:36
  250.1 0.6 dynamic_slice.23
  253.9 4.4 %fusion.23 = f32[16,1270,128]{2,1,0:T(8,128)} fusion(f32[16,1270,128]{2,1,0:T(8,128)} %get-tuple-element.88, s32[]{:T(128)} %get-tuple-element.87, bf16[1270,3072]{1,0:T(8,128)(2,1)} %get-tuple-element.99, s32[]{:T(128)S(6)} %select_n.44, bf16[1152,2048]{1,0:T(8,128)(2,1)} %get-tuple-element.100, s32[]{:T(128)S(6)} %select_n.45), kind=kOutput, calls=%fused_computation.4.clone.1 | convolution fusion | flops 374538240 | bytes 3877384 | tf_op jit(solution)/shard_map/while/body/eval_jaxpr/dot_general | solution.py:36
  258.3 0.6 dynamic_slice.23
  262.1 4.4 %fusion.23 = f32[16,1270,128]{2,1,0:T(8,128)} fusion(f32[16,1270,128]{2,1,0:T(8,128)} %get-tuple-element.88, s32[]{:T(128)} %get-tuple-element.87, bf16[1270,3072]{1,0:T(8,128)(2,1)} %get-tuple-element.99, s32[]{:T(128)S(6)} %select_n.44, bf16[1152,2048]{1,0:T(8,128)(2,1)} %get-tuple-element.100, s32[]{:T(128)S(6)} %select_n.45), kind=kOutput, calls=%fused_computation.4.clone.1 | convolution fusion | flops 374538240 | bytes 3877384 | tf_op jit(solution)/shard_map/while/body/eval_jaxpr/dot_general | solution.py:36
  266.5 0.6 dynamic_slice.23
  270.2 4.4 %fusion.23 = f32[16,1270,128]{2,1,0:T(8,128)} fusion(f32[16,1270,128]{2,1,0:T(8,128)} %get-tuple-element.88, s32[]{:T(128)} %get-tuple-element.87, bf16[1270,3072]{1,0:T(8,128)(2,1)} %get-tuple-element.99, s32[]{:T(128)S(6)} %select_n.44, bf16[1152,2048]{1,0:T(8,128)(2,1)} %get-tuple-element.100, s32[]{:T(128)S(6)} %select_n.45), kind=kOutput, calls=%fused_computation.4.clone.1 | convolution fusion | flops 374538240 | bytes 3877384 | tf_op jit(solution)/shard_map/while/body/eval_jaxpr/dot_general | solution.py:36
  274.7 0.6 dynamic_slice.23
  278.4 4.3 %fusion.23 = f32[16,1270,128]{2,1,0:T(8,128)} fusion(f32[16,1270,128]{2,1,0:T(8,128)} %get-tuple-element.88, s32[]{:T(128)} %get-tuple-element.87, bf16[1270,3072]{1,0:T(8,128)(2,1)} %get-tuple-element.99, s32[]{:T(128)S(6)} %select_n.44, bf16[1152,2048]{1,0:T(8,128)(2,1)} %get-tuple-element.100, s32[]{:T(128)S(6)} %select_n.45), kind=kOutput, calls=%fused_computation.4.clone.1 | convolution fusion | flops 374538240 | bytes 3877384 | tf_op jit(solution)/shard_map/while/body/eval_jaxpr/dot_general | solution.py:36
  282.8 0.6 dynamic_slice.23
  286.5 4.4 %fusion.23 = f32[16,1270,128]{2,1,0:T(8,128)} fusion(f32[16,1270,128]{2,1,0:T(8,128)} %get-tuple-element.88, s32[]{:T(128)} %get-tuple-element.87, bf16[1270,3072]{1,0:T(8,128)(2,1)} %get-tuple-element.99, s32[]{:T(128)S(6)} %select_n.44, bf16[1152,2048]{1,0:T(8,128)(2,1)} %get-tuple-element.100, s32[]{:T(128)S(6)} %select_n.45), kind=kOutput, calls=%fused_computation.4.clone.1 | convolution fusion | flops 374538240 | bytes 3877384 | tf_op jit(solution)/shard_map/while/body/eval_jaxpr/dot_general | solution.py:36
  290.9 0.6 dynamic_slice.23
  294.7 4.4 %fusion.23 = f32[16,1270,128]{2,1,0:T(8,128)} fusion(f32[16,1270,128]{2,1,0:T(8,128)} %get-tuple-element.88, s32[]{:T(128)} %get-tuple-element.87, bf16[1270,3072]{1,0:T(8,128)(2,1)} %get-tuple-element.99, s32[]{:T(128)S(6)} %select_n.44, bf16[1152,2048]{1,0:T(8,128)(2,1)} %get-tuple-element.100, s32[]{:T(128)S(6)} %select_n.45), kind=kOutput, calls=%fused_computation.4.clone.1 | convolution fusion | flops 374538240 | bytes 3877384 | tf_op jit(solution)/shard_map/while/body/eval_jaxpr/dot_general | solution.py:36
  299.0 0.6 dynamic_slice.23
  302.8 4.3 %fusion.23 = f32[16,1270,128]{2,1,0:T(8,128)} fusion(f32[16,1270,128]{2,1,0:T(8,128)} %get-tuple-element.88, s32[]{:T(128)} %get-tuple-element.87, bf16[1270,3072]{1,0:T(8,128)(2,1)} %get-tuple-element.99, s32[]{:T(128)S(6)} %select_n.44, bf16[1152,2048]{1,0:T(8,128)(2,1)} %get-tuple-element.100, s32[]{:T(128)S(6)} %select_n.45), kind=kOutput, calls=%fused_computation.4.clone.1 | convolution fusion | flops 374538240 | bytes 3877384 | tf_op jit(solution)/shard_map/while/body/eval_jaxpr/dot_general | solution.py:36
  307.2 0.6 dynamic_slice.23
  310.9 4.1 %fusion.23 = f32[16,1270,128]{2,1,0:T(8,128)} fusion(f32[16,1270,128]{2,1,0:T(8,128)} %get-tuple-element.88, s32[]{:T(128)} %get-tuple-element.87, bf16[1270,3072]{1,0:T(8,128)(2,1)} %get-tuple-element.99, s32[]{:T(128)S(6)} %select_n.44, bf16[1152,2048]{1,0:T(8,128)(2,1)} %get-tuple-element.100, s32[]{:T(128)S(6)} %select_n.45), kind=kOutput, calls=%fused_computation.4.clone.1 | convolution fusion | flops 374538240 | bytes 3877384 | tf_op jit(solution)/shard_map/while/body/eval_jaxpr/dot_general | solution.py:36
  315.0 11.8 %copy.12 = f32[1270,16,128]{2,1,0:T(8,128)} copy(f32[1270,16,128]{2,0,1:T(8,128)} %bitcast.30) | data formatting | bytes 20807680 | tf_op jit(solution)/shard_map/transpose | solution.py:39
  326.8 10.2 %reshape_reshape.3 = f32[10,127,2048]{2,1,0:T(8,128)} reshape(f32[1270,16,128]{2,1,0:T(8,128)} %copy.12) | data formatting | bytes 20807680 | tf_op jit(solution)/shard_map/reshape;reshape | solution.py:57
  337.0 0.0 copy-done
  337.0 0.0 copy-start.1
  337.0 10.0 %fusion.10 = f32[10,2048,40]{1,2,0:T(8,128)S(1)} fusion(f32[10,127,2048]{2,1,0:T(8,128)} %reshape_reshape.3, bf16[127,40]{0,1:T(8,128)(2,1)S(1)} %copy-done), kind=kOutput, calls=%fused_computation.10 | convolution fusion | flops 218480640 | bytes 13690800 | tf_op jit(solution)/shard_map/lm,klc->kmc/dot_general | solution.py:61
  347.0 0.0 copy-done.1
  347.0 3.2 add_bitcast_fusion
  (5 shorter events, 0.1 us)
Async XLA Ops:
  6.5 330.5 %copy-start = (bf16[127,40]{0,1:T(8,128)(2,1)S(1)}, bf16[127,40]{0,1:T(8,128)(2,1)}, u32[]{:S(2)}) copy-start(bf16[127,40]{0,1:T(8,128)(2,1)} %param.9) | copy-start | bytes 30484
  6.5 103.0 %all-gather.2.cloned.1.call-start = ((), (), s32[]{:S(2)}) async-start(), calls=%async_computation.1 | async-start | bytes 4718592 | tf_op jit(solution)/shard_map/all_gather | solution.py:47
  150.4 10.0 %copy-start.2 = (s32[2,1]{0,1:T(1,128)S(1)}, s32[2,1]{0,1:T(1,128)}, u32[]{:S(2)}) copy-start(s32[2,1]{0,1:T(1,128)} %param.13) | copy-start | bytes 28
  158.1 16.8 %collective-permute-start = (bf16[1270,512]{1,0:T(8,128)(2,1)S(1)}, bf16[1270,512]{1,0:T(8,128)(2,1)}, u32[]{:S(2)}, u32[]{:S(2)}) collective-permute-start(bf16[1270,512]{1,0:T(8,128)(2,1)S(1)} %get-tuple-element.43), channel_id=1, source_target_pairs={{0,1},{1,2},{2,3},{3,4},{4,5},{5,6},{6,7},{7,8},{8,9},{9,10},{10,1... | collective-permute-start | bytes 3901448 | tf_op jit(solution)/shard_map/ppermute | solution.py:16
  160.4 17.3 %collective-permute-start.1 = (bf16[1270,512]{1,0:T(8,128)(2,1)S(1)}, bf16[1270,512]{1,0:T(8,128)(2,1)}, u32[]{:S(2)}, u32[]{:S(2)}) collective-permute-start(bf16[1270,512]{1,0:T(8,128)(2,1)S(1)} %get-tuple-element.44), channel_id=1, source_target_pairs={{1,0},{2,1},{3,2},{4,3},{5,4},{6,5},{7,6},{8,7},{9,8},{10,9},{11,1... | collective-permute-start | bytes 3901448 | tf_op jit(solution)/shard_map/ppermute | solution.py:19
  337.0 10.0 %copy-start.1 = (f32[10,127,2048]{2,1,0:T(8,128)S(1)}, f32[10,127,2048]{2,1,0:T(8,128)}, u32[]{:S(2)}) copy-start(f32[10,127,2048]{2,1,0:T(8,128)} %reshape_reshape.3) | copy-start | bytes 31211524
Sparse Core Ops, SparseCore 0:
  35.5 74.0 all-gather.1
where the time goes:
time: 358 us; the launch traced here: 357 us
  waiting for transfers between devices  88.2 us (25%)
  matrix products  82.7 us (23%)
  local copies, waits for them, and re-layouts  73.1 us (20%)
  loops' own time  49.9 us (14%)
  blocking collectives  27.5 us (8%)
  other arithmetic  18.7 us (5%)
  between operations  14.6 us (4%)
    all_gather x1, waiting for transfers between devices, local(): gathered = lax.all_gather(relayed, 'mem', axis=1, tiled=True)  72.6 us
    dot_general x16, matrix products, one_tile(): return jnp.dot(window, weights, preferred_element_type=jnp.float32)  69.6 us
    another operation x1, loops' own time, smooth(): lax.map(one_tile, jnp.arange(tile_count, dtype=jnp.int32) * TILE)  49.9 us
    gather x1, local copies, waits for them, and re-layouts, local(): jnp.take(gathered, child_map.reshape(-1), axis=1)  30.1 us
    all_to_all x1, blocking collectives, local(): lax.all_to_all(grad_hi, 'space', split_axis=1, concat_axis=1, tiled=True)  27.5 us
    ppermute x1, waiting for transfers between devices, padded(): lax.ppermute(lax.slice_in_dim(block, block.shape[dim] - width, None, axis...  12.7 us
    transpose x1, local copies, waits for them, and re-layouts, smooth(): tile_results.transpose(1, 0, 2).reshape(extended.shape[0], cell_count)  11.8 us
    dynamic_slice x16, local copies, waits for them, and re-layouts, smooth(): lax.map(one_tile, jnp.arange(tile_count, dtype=jnp.int32) * TILE)  10.3 us
  transfers between devices with their start and end apart: 3, of which 3 were waited for; matrix products, arithmetic and copies ran while one was open for 1% of the time, Pallas kernels for 0%

commit v1 on v0

v1 whole, which is shorter than its diff:
```python
import jax
import jax.numpy as jnp
from jax import lax
from jax.experimental import pallas as pl
from jax.experimental.pallas import tpu as pltpu
from jax.sharding import PartitionSpec as P

MESH = pl.DeviceIdType.MESH
BF16 = jnp.bfloat16
F32 = jnp.float32

TILE = 128
HALO = 512
LEV = 127
LEV_PAD = 128
MODES = 40
CELLS = 2048
EXT = CELLS + 2 * HALO
N_MEM = 8
N_SPACE = 32
CHUNK = LEV_PAD // N_MEM
HI = 1024
SEND = HI // N_SPACE
CODES = 512
GROUPS = N_MEM * HI // CODES
EDGE = 2 * HALO
PAIRS = 5
ROWS = 2 * MODES


def remote(src, dst, send, recv, mem, space):
    return pltpu.make_async_remote_copy(
        src_ref=src,
        dst_ref=dst,
        send_sem=send,
        recv_sem=recv,
        device_id=(mem, space),
        device_id_type=MESH,
    )


def reduce_kernel(
    grad, child, modes, ens_hbm, out_hbm,
    gb, got_levels, turned, got_cols, picker, coarse_edge, coarse_mid, ens, prod, modes_pad, modes_two, red,
    ens_sem, m_send, m_recv, s_send, s_recv, e_send, e_recv, c_send, c_recv, h_send, h_recv, out_sem,
):
    mem = lax.axis_index("mem")
    space = lax.axis_index("space")
    mem_at = lambda d: lax.rem(mem + d, N_MEM)
    space_at = lambda d: lax.rem(space + d, N_SPACE)

    ens_copy = pltpu.make_async_copy(ens_hbm, ens, ens_sem)
    ens_copy.start()

    barrier = pltpu.get_barrier_semaphore()

    @pl.loop(1, N_MEM)
    def _(d):
        pl.semaphore_signal(barrier, inc=1, device_id=(mem_at(d), space), device_id_type=MESH)

    @pl.loop(1, N_SPACE)
    def _(d):
        pl.semaphore_signal(barrier, inc=1, device_id=(mem, space_at(d)), device_id_type=MESH)

    for m in range(N_MEM - 1):
        gb[m] = grad[m * CHUNK : (m + 1) * CHUNK, :].astype(BF16)
    last = grad[(N_MEM - 1) * CHUNK : LEV, :]
    gb[N_MEM - 1] = jnp.concatenate([last, jnp.zeros((1, HI), F32)], axis=0).astype(BF16)

    pl.semaphore_wait(barrier, N_MEM - 1 + N_SPACE - 1)

    def level_copy(d):
        target = mem_at(d)
        return remote(gb.at[target], got_levels.at[mem], m_send.at[d], m_recv.at[d], target, space)

    @pl.loop(1, N_MEM)
    def _(d):
        level_copy(d).start()

    got_levels[mem] = gb[mem]

    modes_pad[...] = jnp.zeros_like(modes_pad)
    modes_pad[0:LEV, 0:MODES] = modes[...].astype(F32)
    flipped = modes_pad[...].T[0:MODES, :]
    modes_two[...] = jnp.zeros_like(modes_two)
    modes_two[0:MODES, 0:LEV_PAD] = flipped
    modes_two[MODES:ROWS, LEV_PAD : 2 * LEV_PAD] = flipped
    prod[...] = jnp.zeros_like(prod)

    @pl.loop(1, N_MEM)
    def _(d):
        level_copy(d).wait()

    for q in range(HI // 128):
        part = got_levels[:, :, q * 128 : (q + 1) * 128].reshape(LEV_PAD, 128)
        turned[q * 4 : (q + 1) * 4] = part.T.reshape(4, SEND, LEV_PAD)

    def column_copy(d):
        target = space_at(d)
        return remote(turned.at[target], got_cols.at[space], s_send.at[d], s_recv.at[d], mem, target)

    @pl.loop(1, N_SPACE)
    def _(d):
        column_copy(d).start()

    got_cols[space] = turned[space]

    @pl.loop(0, 4 * CELLS // 256)
    def _(t):
        j = t // (CELLS // 256)
        first = pl.multiple_of(lax.rem(t, CELLS // 256) * 256, 256)
        low = child[pl.ds(j, 1), pl.ds(first, 256)] & (CODES - 1)
        hot = lax.broadcasted_iota(jnp.int32, (CODES, 256), 0) == low
        picker[:, pl.ds(pl.multiple_of(t * 256, 256), 256)] = hot.astype(F32).astype(BF16)

    @pl.loop(1, N_SPACE)
    def _(d):
        column_copy(d).wait()

    halves = []
    for h in range(2):
        cols = got_cols[h * 16 : (h + 1) * 16].reshape(CODES, LEV_PAD)
        halves.append(cols.T)
    table = jnp.concatenate(halves, axis=0)

    def pick(first, width):
        total = jnp.zeros((CHUNK, width), F32)
        for j in range(4):
            found = jnp.dot(
                table, picker[:, j * CELLS + first : j * CELLS + first + width], preferred_element_type=F32
            )
            code = child[j : j + 1, first : first + width]
            group = ((code >> 9) & 1) * N_MEM + (code >> 10)
            for g in range(GROUPS):
                total = total + jnp.where(group == g, found[g * CHUNK : (g + 1) * CHUNK, :], 0.0)
        return (0.25 * total).astype(BF16)

    def edge_copy(d):
        return remote(coarse_edge.at[mem], coarse_edge.at[mem], e_send.at[d], e_recv.at[d], mem_at(d), space)

    def mid_copy(d):
        return remote(coarse_mid.at[mem], coarse_mid.at[mem], c_send.at[d], c_recv.at[d], mem_at(d), space)

    coarse_edge[mem, :, 0:HALO] = pick(0, HALO)
    coarse_edge[mem, :, HALO:EDGE] = pick(CELLS - HALO, HALO)

    @pl.loop(1, N_MEM)
    def _(d):
        edge_copy(d).start()

    coarse_mid[mem, :, 0:HALO] = pick(HALO, HALO)
    coarse_mid[mem, :, HALO:EDGE] = pick(2 * HALO, HALO)

    @pl.loop(1, N_MEM)
    def _(d):
        mid_copy(d).start()

    two = modes_two[...].astype(BF16)

    def reduced(pair, cells, coarse):
        for i in range(2):
            prod[i * LEV_PAD : i * LEV_PAD + LEV, :] = ens[2 * pair + i, :, cells : cells + HALO] * coarse
        return jnp.dot(two, prod[...], preferred_element_type=F32).astype(BF16)

    def to_lower(pair):
        rows = pl.ds(pair * ROWS, ROWS)
        return remote(
            red.at[rows, pl.ds(HALO, HALO)], red.at[rows, pl.ds(HALO + CELLS, HALO)],
            h_send.at[0, pair], h_recv.at[0, pair], mem, space_at(N_SPACE - 1),
        )

    def to_upper(pair):
        rows = pl.ds(pair * ROWS, ROWS)
        return remote(
            red.at[rows, pl.ds(CELLS, HALO)], red.at[rows, pl.ds(0, HALO)],
            h_send.at[1, pair], h_recv.at[1, pair], mem, space_at(1),
        )

    ens_copy.wait()

    @pl.loop(1, N_MEM)
    def _(d):
        edge_copy(d).wait()

    low = coarse_edge[:, :, 0:HALO].reshape(LEV_PAD, HALO)[0:LEV]
    high = coarse_edge[:, :, HALO:EDGE].reshape(LEV_PAD, HALO)[0:LEV]
    for pair in range(PAIRS):
        rows = slice(pair * ROWS, (pair + 1) * ROWS)
        red[rows, HALO : 2 * HALO] = reduced(pair, 0, low)
        to_lower(pair).start()
        red[rows, CELLS : CELLS + HALO] = reduced(pair, CELLS - HALO, high)
        to_upper(pair).start()

    @pl.loop(1, N_MEM)
    def _(d):
        mid_copy(d).wait()

    for half in range(2):
        coarse = coarse_mid[:, :, half * HALO : (half + 1) * HALO].reshape(LEV_PAD, HALO)[0:LEV]
        cells = HALO * (1 + half)
        for pair in range(PAIRS):
            red[pair * ROWS : (pair + 1) * ROWS, HALO + cells : 2 * HALO + cells] = reduced(pair, cells, coarse)

    def out_copy(i, first, width):
        return pltpu.make_async_copy(
            red.at[:, pl.ds(first, width)], out_hbm.at[:, pl.ds(first, width)], out_sem.at[i]
        )

    copies = [out_copy(0, HALO, CELLS), out_copy(1, 0, HALO), out_copy(2, HALO + CELLS, HALO)]
    copies[0].start()
    for pair in range(PAIRS):
        to_lower(pair).wait()
        to_upper(pair).wait()
    copies[1].start()
    copies[2].start()
    for copy in copies:
        copy.wait()


def smooth_kernel(halo_rows, ext, stencil, out, window, weights, sems):
    t = pl.program_id(0)
    span = 2 * TILE + 2 * HALO

    def load(tile, side):
        return pltpu.make_async_copy(
            stencil.at[:, pl.ds(tile * 2 * TILE + side * TILE, TILE)],
            weights.at[tile, pl.ds(side * TILE, TILE + 2 * HALO), pl.ds(side * TILE, TILE)],
            sems.at[tile, side],
        )

    @pl.when(t == 0)
    def _():
        for tile in range(CELLS // (2 * TILE)):
            for side in range(2):
                load(tile, side).start()
        for tile in range(CELLS // (2 * TILE)):
            weights[tile, span - TILE : span, 0:TILE] = jnp.zeros((TILE, TILE), BF16)
            weights[tile, 0:TILE, TILE : 2 * TILE] = jnp.zeros((TILE, TILE), BF16)
        col = lax.broadcasted_iota(jnp.int32, (5 * ROWS, HALO), 1)
        window[:, HALO : HALO + CELLS] = ext[:, HALO : HALO + CELLS]
        low = ext[:, 0:HALO].astype(F32)
        window[:, 0:HALO] = jnp.where(col >= HALO - halo_rows[0, 0], low, 0.0).astype(BF16)
        high = ext[:, HALO + CELLS : EXT].astype(F32)
        window[:, HALO + CELLS : EXT] = jnp.where(col < halo_rows[1, 0], high, 0.0).astype(BF16)

    load(t, 0).wait()
    load(t, 1).wait()
    first = pl.multiple_of(t * 2 * TILE, 2 * TILE)
    out[...] = jnp.dot(window[:, pl.ds(first, span)], weights[t], preferred_element_type=F32)


def local(ens_pert, vert_modes, loc_stencil, grad_hi, child_map, halo_rows):
    vmem = pl.BlockSpec(memory_space=pltpu.VMEM)
    anywhere = pl.BlockSpec(memory_space=pl.ANY)
    dma = pltpu.SemaphoreType.DMA
    rows = PAIRS * ROWS
    ext = pl.pallas_call(
        reduce_kernel,
        out_shape=jax.ShapeDtypeStruct((rows, EXT), BF16),
        in_specs=[vmem, vmem, vmem, anywhere],
        out_specs=anywhere,
        scratch_shapes=[
            pltpu.VMEM((N_MEM, CHUNK, HI), BF16),
            pltpu.VMEM((N_MEM, CHUNK, HI), BF16),
            pltpu.VMEM((N_SPACE, SEND, LEV_PAD), BF16),
            pltpu.VMEM((N_SPACE, SEND, LEV_PAD), BF16),
            pltpu.VMEM((CODES, 4 * CELLS), BF16),
            pltpu.VMEM((N_MEM, CHUNK, EDGE), BF16),
            pltpu.VMEM((N_MEM, CHUNK, EDGE), BF16),
            pltpu.VMEM((2 * PAIRS, LEV, CELLS), BF16),
            pltpu.VMEM((2 * LEV_PAD, HALO), BF16),
            pltpu.VMEM((LEV_PAD, 128), F32),
            pltpu.VMEM((ROWS, 2 * LEV_PAD), F32),
            pltpu.VMEM((rows, EXT), BF16),
            dma,
            dma((N_MEM,)),
            dma((N_MEM,)),
            dma((N_SPACE,)),
            dma((N_SPACE,)),
            dma((N_MEM,)),
            dma((N_MEM,)),
            dma((N_MEM,)),
            dma((N_MEM,)),
            dma((2, PAIRS)),
            dma((2, PAIRS)),
            dma((3,)),
        ],
        compiler_params=pltpu.CompilerParams(
            collective_id=0, has_side_effects=True, vmem_limit_bytes=40 * 2**20
        ),
        name="reduce",
    )(grad_hi, child_map, vert_modes, ens_pert)

    out = pl.pallas_call(
        smooth_kernel,
        grid=(CELLS // (2 * TILE),),
        out_shape=jax.ShapeDtypeStruct((rows, CELLS), F32),
        in_specs=[
            pl.BlockSpec(memory_space=pltpu.SMEM),
            vmem,
            anywhere,
        ],
        out_specs=pl.BlockSpec((rows, 2 * TILE), lambda t: (0, t)),
        scratch_shapes=[
            pltpu.VMEM((rows, EXT), BF16),
            pltpu.VMEM((CELLS // (2 * TILE), 2 * TILE + 2 * HALO, 2 * TILE), BF16),
            dma((CELLS // (2 * TILE), 2)),
        ],
        compiler_params=pltpu.CompilerParams(vmem_limit_bytes=40 * 2**20),
        name="smooth",
    )(halo_rows, ext, loc_stencil)
    return out.reshape(2 * PAIRS, MODES, CELLS)


def solution(mesh):
    placed = (
        P("mem", None, "space"),
        P(),
        P(None, "space"),
        P(None, ("mem", "space")),
        P(None, "space"),
        P(None, "space"),
    )
    return jax.shard_map(
        local, mesh=mesh, in_specs=placed, out_specs=P("mem", None, "space"), check_vma=False
    )
```

time: 358 us -> 54.5 us (0.15)
  waiting for transfers between devices: 88.2 us -> 0 us
  matrix products: 82.7 us -> 0 us
  local copies, waits for them, and re-layouts: 73.1 us -> 5.86 us
  loops' own time: 49.9 us -> 0 us
  Pallas kernels: 0 us -> 48.3 us
  blocking collectives: 27.5 us -> 0 us
  other arithmetic: 18.7 us -> 0 us
  between operations: 14.6 us -> 0.03 us
    dot_general x18 -> x0, matrix products: 82.7 us -> none  [the longest x16 69.6 us: one_tile(): return jnp.dot(window, weights, preferred_element_type=jnp.float32)]
    all_gather x1 -> x0, waiting for transfers between devices: 72.6 us -> none  [local(): gathered = lax.all_gather(relayed, 'mem', axis=1, tiled=True)]
    another operation x1 -> x0, loops' own time: 49.9 us -> none  [smooth(): lax.map(one_tile, jnp.arange(tile_count, dtype=jnp.int32) * TILE)]
    pallas_call x0 -> x2, Pallas kernels: none -> 48.3 us  [the longest x1 40.6 us: local(): pl.pallas_call(reduce_kernel, out_shape=jax.ShapeDtypeStruct((rows, EXT),...]
    gather x1 -> x0, local copies, waits for them, and re-layouts: 30.1 us -> none  [local(): jnp.take(gathered, child_map.reshape(-1), axis=1)]
    all_to_all x1 -> x0, blocking collectives: 27.5 us -> none  [local(): lax.all_to_all(grad_hi, 'space', split_axis=1, concat_axis=1, tiled=True)]
    ppermute x2 -> x0, waiting for transfers between devices: 15.6 us -> none  [the longest x1 12.7 us: padded(): lax.ppermute(lax.slice_in_dim(block, block.shape[dim] - width, None, axis...]
    transpose x1 -> x0, local copies, waits for them, and re-layouts: 11.8 us -> none  [smooth(): tile_results.transpose(1, 0, 2).reshape(extended.shape[0], cell_count)]
  transfers between devices with their start and end apart: 3 -> 0, of which waited for: 3 -> 0; matrix products, arithmetic and copies ran while one was open for 1% -> 0% of each run, Pallas kernels for 0% -> 0%
where the time goes in v1:
time: 54.5 us; the launch traced here: 54.2 us
  Pallas kernels  48.3 us (89%)
  local copies, waits for them, and re-layouts  5.86 us (11%)
    pallas_call x1, Pallas kernels, local(): pl.pallas_call(reduce_kernel, out_shape=jax.ShapeDtypeStruct((rows, EXT),...  40.6 us
    pallas_call x1, Pallas kernels, local(): pl.pallas_call(smooth_kernel, grid=(CELLS // (2 * TILE),), out_shape=jax....  7.65 us
    unnamed x10, local copies, waits for them, and re-layouts  5.86 us

profile of v1, /device:TPU:1, one launch (start us, length us, event | category | flops | bytes accessed | tf_op | source)
XLA Modules:
  0.0 54.2 jit_solution(11340518219243793368)
XLA Ops:
  0.0 0.7 %copy.8.halo_rows = s32[2,1]{1,0:T(2,128)S(1)} copy(s32[2,1]{0,1:T(1,128)} %param.11) | data formatting | bytes 16 | tf_op args[5]
  0.7 0.8 %copy.7.modes = bf16[127,40]{1,0:T(8,128)(2,1)S(1)} copy(bf16[127,40]{0,1:T(8,128)(2,1)} %param.7) | data formatting | bytes 20320 | tf_op args[1]
  1.6 0.0 copy-start
  1.6 2.5 %copy-done = bf16[10,127,2048]{2,1,0:T(8,128)(2,1)S(1)} copy-done((bf16[10,127,2048]{2,1,0:T(8,128)(2,1)S(1)}, bf16[10,127,2048]{2,1,0:T(8,128)(2,1)}, u32[]{:S(2)}) %copy-start) | copy-done | bytes 5201944
  4.1 0.0 copy-start.2
  4.1 1.0 %copy-done.2 = f32[127,1024]{1,0:T(8,128)S(1)} copy-done((f32[127,1024]{1,0:T(8,128)S(1)}, f32[127,1024]{1,0:T(8,128)}, u32[]{:S(2)}) %copy-start.2) | copy-done | bytes 520216
  5.1 0.0 copy-start.3
  5.1 0.8 %copy-done.3 = s32[4,2048]{1,0:T(4,128)S(1)} copy-done((s32[4,2048]{1,0:T(4,128)S(1)}, s32[4,2048]{1,0:T(4,128)}, u32[]{:S(2)}) %copy-start.3) | copy-done | bytes 32792
  5.9 0.0 copy-start.1
  5.9 40.6 %reduce.1.ext = bf16[400,3072]{1,0:T(8,128)(2,1)S(1)} custom-call(f32[127,1024]{1,0:T(8,128)S(1)} %copy-done.2, s32[4,2048]{1,0:T(4,128)S(1)} %copy-done.3, bf16[127,40]{1,0:T(8,128)(2,1)S(1)} %copy.7.modes, bf16[10,127,2048]{2,1,0:T(8,128)(2,1)S(1)} %copy-done), custom_call_target="tpu_custom_call" | custom-call | tf_op jit(solution)/shard_map/reduce/pallas_call | solution.py:257
  46.5 0.0 copy-done.1
  46.5 7.6 %smooth.1 = f32[400,2048]{1,0:T(8,128)} custom-call(s32[2,1]{1,0:T(2,128)S(1)} %copy.8.halo_rows, bf16[400,3072]{1,0:T(8,128)(2,1)S(1)} %reduce.1.ext, bf16[1152,2048]{1,0:T(8,128)(2,1)S(1)} %copy-done.1), custom_call_target="tpu_custom_call" | custom-call | tf_op jit(solution)/shard_map/smooth/pallas_call | solution.py:294
Async XLA Ops:
  1.6 2.5 %copy-start = (bf16[10,127,2048]{2,1,0:T(8,128)(2,1)S(1)}, bf16[10,127,2048]{2,1,0:T(8,128)(2,1)}, u32[]{:S(2)}) copy-start(bf16[10,127,2048]{2,1,0:T(8,128)(2,1)} %ens_hbm.1) | copy-start | bytes 15605764
  4.1 1.0 %copy-start.2 = (f32[127,1024]{1,0:T(8,128)S(1)}, f32[127,1024]{1,0:T(8,128)}, u32[]{:S(2)}) copy-start(f32[127,1024]{1,0:T(8,128)} %grad.1) | copy-start | bytes 1560580
  5.1 0.8 %copy-start.3 = (s32[4,2048]{1,0:T(4,128)S(1)}, s32[4,2048]{1,0:T(4,128)}, u32[]{:S(2)}) copy-start(s32[4,2048]{1,0:T(4,128)} %child.1) | copy-start | bytes 98308
  5.9 40.7 %copy-start.1 = (bf16[1152,2048]{1,0:T(8,128)(2,1)S(1)}, bf16[1152,2048]{1,0:T(8,128)(2,1)}, u32[]{:S(2)}) copy-start(bf16[1152,2048]{1,0:T(8,128)(2,1)} %stencil.1) | copy-start | bytes 14155780

commit v2 on v0

v2 whole, which is shorter than its diff:
```python
import jax
import jax.numpy as jnp
from jax import lax
from jax.experimental import pallas as pl
from jax.experimental.pallas import tpu as pltpu
from jax.sharding import PartitionSpec as P

MESH = pl.DeviceIdType.MESH
BF16 = jnp.bfloat16
F32 = jnp.float32

TILE = 128
HALO = 512
LEV = 127
LEV_PAD = 128
MODES = 40
CELLS = 2048
EXT = CELLS + 2 * HALO
N_MEM = 8
N_SPACE = 32
CHUNK = LEV_PAD // N_MEM
HI = 1024
SEND = HI // N_SPACE
CODES = 512
GROUPS = N_MEM * HI // CODES
PAIRS = 5
ROWS = 2 * MODES
ALL_ROWS = PAIRS * ROWS
MID = CELLS - 2 * HALO
PART = 2 * TILE
SPAN = PART + 2 * HALO

MEM_STEPS = ((2, 1), (1, 1), (3, 1), (0, 1), (2, 0), (1, 0), (3, 0))
Z_STEPS = (4, 3, 5, 2, 6, 1, 7, 0)
OWN_STEPS = [(z, c) for z in Z_STEPS for c in (1, 0) if z or c]
OTHER_STEPS = [(z, c) for z in Z_STEPS for c in (1, 0)]


def remote(src, dst, send, recv, mem, space):
    return pltpu.make_async_remote_copy(
        src_ref=src,
        dst_ref=dst,
        send_sem=send,
        recv_sem=recv,
        device_id=(mem, space),
        device_id_type=MESH,
    )


def paired(even, odd):
    blank = jnp.zeros((TILE, TILE), even.dtype)
    return jnp.concatenate(
        [jnp.concatenate([even, blank], axis=0), jnp.concatenate([blank, odd], axis=0)], axis=1
    )


def reduce_kernel(
    grad_hbm, child_hbm, modes_hbm, ens_hbm, stencil_hbm, red, mid_out,
    grad, child, modes, ens, stencil, gb, got_levels, turned, got_cols, table, picker,
    coarse_far, coarse_rest, prod, modes_two,
    in_sem, m_send, m_recv, s_send, s_recv, e_send, e_recv, c_send, c_recv, h_send, h_recv,
):
    mem = lax.axis_index("mem")
    space = lax.axis_index("space")
    y, x_hi = mem // 2, lax.rem(mem, 2)
    x_lo, z, core = space // 16, lax.rem(space // 2, 8), lax.rem(space, 2)

    def mem_at(step):
        return lax.rem(y + step[0], 4) * 2 + lax.rem(x_hi + step[1], 2)

    def space_at(x, step):
        return x * 16 + lax.rem(z + step[0], 8) * 2 + lax.rem(core + step[1], 2)

    loads = [
        pltpu.make_async_copy(src, dst, in_sem.at[i])
        for i, (src, dst) in enumerate(
            (
                (grad_hbm, grad),
                (modes_hbm, modes),
                (child_hbm, child),
                (ens_hbm, ens),
                (stencil_hbm.at[:, pl.ds(HALO, MID)], stencil),
            )
        )
    ]
    for load in loads:
        load.start()

    barrier = pltpu.get_barrier_semaphore()
    for step in OTHER_STEPS:
        pl.semaphore_signal(barrier, inc=1, device_id=(mem, space_at(1 - x_lo, step)), device_id_type=MESH)
    for step in MEM_STEPS:
        pl.semaphore_signal(barrier, inc=1, device_id=(mem_at(step), space), device_id_type=MESH)
    for step in OWN_STEPS:
        pl.semaphore_signal(barrier, inc=1, device_id=(mem, space_at(x_lo, step)), device_id_type=MESH)

    loads[0].wait()
    for m in range(N_MEM - 1):
        gb[m] = grad[m * CHUNK : (m + 1) * CHUNK, :].astype(BF16)
    last = grad[(N_MEM - 1) * CHUNK : LEV, :]
    gb[N_MEM - 1] = jnp.concatenate([last, jnp.zeros((1, HI), F32)], axis=0).astype(BF16)

    pl.semaphore_wait(barrier, N_MEM - 1 + N_SPACE - 1)

    sides = (x_lo, 1 - x_lo)

    def level_copy(k, i):
        target = mem_at(MEM_STEPS[i])
        cols = pl.ds(pl.multiple_of(sides[k] * CODES, CODES), CODES)
        return remote(
            gb.at[target, :, cols], got_levels.at[mem, :, cols], m_send.at[k, i], m_recv.at[k, i], target, space
        )

    for k in range(2):
        for i in range(N_MEM - 1):
            level_copy(k, i).start()

    got_levels[mem] = gb[mem]

    loads[1].wait()
    modes_two[...] = jnp.zeros_like(modes_two)
    wide = modes[...].astype(F32)
    modes_two[0:MODES, 0:LEV] = wide
    modes_two[MODES:ROWS, LEV_PAD : LEV_PAD + LEV] = wide
    prod[...] = jnp.zeros_like(prod)

    def column_copy(k, i):
        target = space_at(sides[k], (OWN_STEPS, OTHER_STEPS)[k][i])
        return remote(turned.at[target], got_cols.at[space], s_send.at[k, i], s_recv.at[k, i], mem, target)

    counts = (len(OWN_STEPS), len(OTHER_STEPS))
    for k in range(2):
        for i in range(N_MEM - 1):
            level_copy(k, i).wait()
        for q in range(CODES // 128):
            first = pl.multiple_of(sides[k] * CODES + q * 128, 128)
            part = got_levels[:, :, pl.ds(first, 128)].reshape(LEV_PAD, 128)
            turned[pl.ds(sides[k] * 16 + q * 4, 4)] = part.T.reshape(4, SEND, LEV_PAD)
        for i in range(counts[k]):
            column_copy(k, i).start()

    got_cols[space] = turned[space]
    loads[2].wait()

    @pl.loop(0, 4 * CELLS // 256)
    def _(t):
        j = t // (CELLS // 256)
        first = pl.multiple_of(lax.rem(t, CELLS // 256) * 256, 256)
        low = child[pl.ds(j, 1), pl.ds(first, 256)] & (CODES - 1)
        hot = lax.broadcasted_iota(jnp.int32, (CODES, 256), 0) == low
        picker[:, pl.ds(pl.multiple_of(t * 256, 256), 256)] = hot.astype(F32).astype(BF16)

    for k in range(2):
        for i in range(counts[k]):
            column_copy(k, i).wait()
        cols = got_cols[pl.ds(sides[k] * 16, 16)].reshape(CODES, LEV_PAD)
        table[pl.ds(pl.multiple_of(sides[k] * LEV_PAD, LEV_PAD), LEV_PAD), :] = cols.T

    def pick(first, width):
        total = jnp.zeros((CHUNK, width), F32)
        for j in range(4):
            cells = pl.ds(pl.multiple_of(j * CELLS + first, HALO), width)
            found = jnp.dot(table[...], picker[:, cells], preferred_element_type=F32)
            code = child[j : j + 1, pl.ds(pl.multiple_of(first, HALO), width)]
            group = ((code >> 9) & 1) * N_MEM + (code >> 10)
            for g in range(GROUPS):
                total = total + jnp.where(group == g, found[g * CHUNK : (g + 1) * CHUNK, :], 0.0)
        return (0.25 * total).astype(BF16)

    def far_copy(i):
        return remote(
            coarse_far.at[mem], coarse_far.at[mem], e_send.at[i], e_recv.at[i], mem_at(MEM_STEPS[i]), space
        )

    def rest_copy(i):
        return remote(
            coarse_rest.at[mem], coarse_rest.at[mem], c_send.at[i], c_recv.at[i], mem_at(MEM_STEPS[i]), space
        )

    far = core * (CELLS - HALO)
    near = (1 - core) * (CELLS - HALO)
    coarse_far[mem] = pick(far, HALO)
    for i in range(N_MEM - 1):
        far_copy(i).start()
    coarse_rest[mem, :, 0:HALO] = pick(near, HALO)
    coarse_rest[mem, :, HALO : 2 * HALO] = pick(HALO, HALO)
    coarse_rest[mem, :, 2 * HALO : 3 * HALO] = pick(2 * HALO, HALO)
    for i in range(N_MEM - 1):
        rest_copy(i).start()

    two = modes_two[...].astype(BF16)

    def reduce_cells(pair, first, coarse):
        for i in range(2):
            pert = ens[2 * pair + i, :, pl.ds(pl.multiple_of(first, HALO), HALO)]
            prod[i * LEV_PAD : i * LEV_PAD + LEV, :] = pert * coarse
        value = jnp.dot(two, prod[...], preferred_element_type=F32).astype(BF16)
        red[pair * ROWS : (pair + 1) * ROWS, pl.ds(pl.multiple_of(HALO + first, HALO), HALO)] = value

    def halo_copy(side, pair):
        rows = pl.ds(pair * ROWS, ROWS)
        first, place, target = (
            (far, (1 - core) * (HALO + CELLS), lax.rem(space + 2 * core + N_SPACE - 1, N_SPACE)),
            (near, core * (HALO + CELLS), space + 1 - 2 * core),
        )[side]
        return remote(
            red.at[rows, pl.ds(pl.multiple_of(HALO + first, HALO), HALO)],
            red.at[rows, pl.ds(pl.multiple_of(place, HALO), HALO)],
            h_send.at[side, pair], h_recv.at[side, pair], mem, target,
        )

    loads[3].wait()
    for i in range(N_MEM - 1):
        far_copy(i).wait()
    coarse = coarse_far[...].reshape(LEV_PAD, HALO)[0:LEV]
    for pair in range(PAIRS):
        reduce_cells(pair, far, coarse)
        halo_copy(0, pair).start()

    for i in range(N_MEM - 1):
        rest_copy(i).wait()
    coarse = coarse_rest[:, :, 0:HALO].reshape(LEV_PAD, HALO)[0:LEV]
    for pair in range(PAIRS):
        reduce_cells(pair, near, coarse)
        halo_copy(1, pair).start()
    for half in range(2):
        coarse = coarse_rest[:, :, (half + 1) * HALO : (half + 2) * HALO].reshape(LEV_PAD, HALO)[0:LEV]
        for pair in range(PAIRS):
            reduce_cells(pair, HALO * (half + 1), coarse)

    loads[4].wait()
    for part in range(MID // PART):
        cells = part * PART
        weights = paired(stencil[:, cells : cells + TILE], stencil[:, cells + TILE : cells + PART])
        window = red[:, HALO + cells : HALO + cells + SPAN]
        mid_out[:, cells : cells + PART] = jnp.dot(window, weights, preferred_element_type=F32)

    for side in range(2):
        for pair in range(PAIRS):
            halo_copy(side, pair).wait()


def edge_kernel(halo_rows, ext, stencil, mid, out, result, sems):
    mid_copy = pltpu.make_async_copy(mid, out.at[:, pl.ds(HALO, MID)], sems.at[0])
    mid_copy.start()
    copies = [mid_copy]

    col = lax.broadcasted_iota(jnp.int32, (16, HALO), 1)
    low_kept = (col >= HALO - halo_rows[0, 0]).astype(F32).astype(BF16)[0:1]
    high_kept = (col < halo_rows[0, 1]).astype(F32).astype(BF16)[0:1]
    low = ext[:, 0:HALO] * low_kept
    high = ext[:, HALO + CELLS : EXT] * high_kept

    for n, part in enumerate((0, 1, CELLS // PART - 2, CELLS // PART - 1)):
        cells = part * PART
        if part < 2:
            window = jnp.concatenate([low[:, cells:], ext[:, HALO : cells + SPAN]], axis=1)
        else:
            window = jnp.concatenate(
                [ext[:, cells : HALO + CELLS], high[:, 0 : cells + SPAN - HALO - CELLS]], axis=1
            )
        weights = paired(stencil[:, cells : cells + TILE], stencil[:, cells + TILE : cells + PART])
        result[n] = jnp.dot(window, weights, preferred_element_type=F32)
        copy = pltpu.make_async_copy(result.at[n], out.at[:, pl.ds(cells, PART)], sems.at[n + 1])
        copy.start()
        copies.append(copy)
    for copy in copies:
        copy.wait()


def local(ens_pert, vert_modes, loc_stencil, grad_hi, child_map, halo_rows):
    vmem = pl.BlockSpec(memory_space=pltpu.VMEM)
    hbm = pl.BlockSpec(memory_space=pltpu.HBM)
    anywhere = pl.BlockSpec(memory_space=pl.ANY)
    dma = pltpu.SemaphoreType.DMA
    held = [
        pltpu.with_memory_space_constraint(x, pltpu.HBM)
        for x in (grad_hi, child_map, vert_modes.T, ens_pert, loc_stencil)
    ]
    ext, mid = pl.pallas_call(
        reduce_kernel,
        out_shape=(
            jax.ShapeDtypeStruct((ALL_ROWS, EXT), BF16),
            jax.ShapeDtypeStruct((ALL_ROWS, MID), F32),
        ),
        in_specs=[hbm] * 5,
        out_specs=(vmem, vmem),
        scratch_shapes=[
            pltpu.VMEM((LEV, HI), F32),
            pltpu.VMEM((4, CELLS), jnp.int32),
            pltpu.VMEM((MODES, LEV), BF16),
            pltpu.VMEM((2 * PAIRS, LEV, CELLS), BF16),
            pltpu.VMEM((TILE + 2 * HALO, MID), BF16),
            pltpu.VMEM((N_MEM, CHUNK, HI), BF16),
            pltpu.VMEM((N_MEM, CHUNK, HI), BF16),
            pltpu.VMEM((N_SPACE, SEND, LEV_PAD), BF16),
            pltpu.VMEM((N_SPACE, SEND, LEV_PAD), BF16),
            pltpu.VMEM((2 * LEV_PAD, CODES), BF16),
            pltpu.VMEM((CODES, 4 * CELLS), BF16),
            pltpu.VMEM((N_MEM, CHUNK, HALO), BF16),
            pltpu.VMEM((N_MEM, CHUNK, 3 * HALO), BF16),
            pltpu.VMEM((2 * LEV_PAD, HALO), BF16),
            pltpu.VMEM((ROWS, 2 * LEV_PAD), F32),
            dma((5,)),
            dma((2, N_MEM)),
            dma((2, N_MEM)),
            dma((2, N_SPACE // 2)),
            dma((2, N_SPACE // 2)),
            dma((N_MEM,)),
            dma((N_MEM,)),
            dma((N_MEM,)),
            dma((N_MEM,)),
            dma((2, PAIRS)),
            dma((2, PAIRS)),
        ],
        compiler_params=pltpu.CompilerParams(
            collective_id=0, has_side_effects=True, vmem_limit_bytes=40 * 2**20
        ),
        name="reduce",
    )(*held)

    out = pl.pallas_call(
        edge_kernel,
        out_shape=jax.ShapeDtypeStruct((ALL_ROWS, CELLS), F32),
        in_specs=[pl.BlockSpec(memory_space=pltpu.SMEM), vmem, vmem, anywhere],
        out_specs=anywhere,
        scratch_shapes=[pltpu.VMEM((4, ALL_ROWS, PART), F32), dma((5,))],
        compiler_params=pltpu.CompilerParams(vmem_limit_bytes=40 * 2**20),
        name="edges",
    )(halo_rows.T, ext, loc_stencil, mid)
    return out.reshape(2 * PAIRS, MODES, CELLS)


def solution(mesh):
    placed = (
        P("mem", None, "space"),
        P(),
        P(None, "space"),
        P(None, ("mem", "space")),
        P(None, "space"),
        P(None, "space"),
    )
    return jax.shard_map(
        local, mesh=mesh, in_specs=placed, out_specs=P("mem", None, "space"), check_vma=False
    )
```

time: 358 us -> 43.6 us (0.12)
  waiting for transfers between devices: 88.2 us -> 0 us
  matrix products: 82.7 us -> 0 us
  local copies, waits for them, and re-layouts: 73.1 us -> 0.01 us
  loops' own time: 49.9 us -> 0 us
  Pallas kernels: 0 us -> 43.5 us
  blocking collectives: 27.5 us -> 0 us
  other arithmetic: 18.7 us -> 0 us
  between operations: 14.6 us -> 0.03 us
    dot_general x18 -> x0, matrix products: 82.7 us -> none  [the longest x16 69.6 us: one_tile(): return jnp.dot(window, weights, preferred_element_type=jnp.float32)]
    all_gather x1 -> x0, waiting for transfers between devices: 72.6 us -> none  [local(): gathered = lax.all_gather(relayed, 'mem', axis=1, tiled=True)]
    another operation x1 -> x0, loops' own time: 49.9 us -> none  [smooth(): lax.map(one_tile, jnp.arange(tile_count, dtype=jnp.int32) * TILE)]
    pallas_call x0 -> x2, Pallas kernels: none -> 43.5 us  [the longest x1 40.8 us: local(): pl.pallas_call(reduce_kernel, out_shape=(jax.ShapeDtypeStruct((ALL_ROWS,...]
    gather x1 -> x0, local copies, waits for them, and re-layouts: 30.1 us -> none  [local(): jnp.take(gathered, child_map.reshape(-1), axis=1)]
    all_to_all x1 -> x0, blocking collectives: 27.5 us -> none  [local(): lax.all_to_all(grad_hi, 'space', split_axis=1, concat_axis=1, tiled=True)]
    ppermute x2 -> x0, waiting for transfers between devices: 15.6 us -> none  [the longest x1 12.7 us: padded(): lax.ppermute(lax.slice_in_dim(block, block.shape[dim] - width, None, axis...]
    transpose x1 -> x0, local copies, waits for them, and re-layouts: 11.8 us -> none  [smooth(): tile_results.transpose(1, 0, 2).reshape(extended.shape[0], cell_count)]
  transfers between devices with their start and end apart: 3 -> 0, of which waited for: 3 -> 0; matrix products, arithmetic and copies ran while one was open for 1% -> 0% of each run, Pallas kernels for 0% -> 0%
where the time goes in v2:
time: 43.6 us; the launch traced here: 43.5 us
  Pallas kernels  43.5 us (100%)
    pallas_call x1, Pallas kernels, local(): pl.pallas_call(reduce_kernel, out_shape=(jax.ShapeDtypeStruct((ALL_ROWS,...  40.8 us
    pallas_call x1, Pallas kernels, local(): pl.pallas_call(edge_kernel, out_shape=jax.ShapeDtypeStruct((ALL_ROWS, CEL...  2.76 us

profile of v2, /device:TPU:1, one launch (start us, length us, event | category | flops | bytes accessed | tf_op | source)
XLA Modules:
  0.0 43.5 jit_solution(9477937932528878585)
XLA Ops:
  0.0 0.0 copy-start
  0.0 0.0 copy-start.1
  0.0 40.8 %reduce.1 = (bf16[400,3072]{1,0:T(8,128)(2,1)S(1)}, f32[400,1024]{1,0:T(8,128)S(1)}) custom-call(f32[127,1024]{1,0:T(8,128)} %grad_hbm.1, s32[4,2048]{1,0:T(4,128)} %child_hbm.1, bf16[40,127]{1,0:T(8,128)(2,1)} %bitcast.4, bf16[10,127,2048]{2,1,0:T(8,128)(2,1)} %ens_hbm.1, bf16[1152,2048]{1,0:T(8,128)(2,1)} %stencil.1), custom_call_target="tpu_custom_call" | custom-call | tf_op jit(solution)/shard_map/reduce/pallas_call | solution.py:280
  40.8 0.0 copy-done
  40.8 0.0 copy-done.1
  40.8 2.8 %edges.1 = f32[400,2048]{1,0:T(8,128)} custom-call(s32[1,2]{1,0:T(1,128)S(1)} %bitcast.3, bf16[400,3072]{1,0:T(8,128)(2,1)S(1)} %get-tuple-element.7.ext, bf16[1152,2048]{1,0:T(8,128)(2,1)S(1)} %copy-done, f32[400,1024]{1,0:T(8,128)S(1)} %get-tuple-element.8.mid), custom_call_target="tpu_custom_call" | custom-call | tf_op jit(solution)/shard_map/edges/pallas_call | solution.py:322
Async XLA Ops:
  0.0 40.8 %copy-start = (bf16[1152,2048]{1,0:T(8,128)(2,1)S(1)}, bf16[1152,2048]{1,0:T(8,128)(2,1)}, u32[]{:S(2)}) copy-start(bf16[1152,2048]{1,0:T(8,128)(2,1)} %stencil.1) | copy-start | bytes 14155780
  0.0 40.8 %copy-start.1 = (s32[2,1]{0,1:T(1,128)S(1)}, s32[2,1]{0,1:T(1,128)}, u32[]{:S(2)}) copy-start(s32[2,1]{0,1:T(1,128)} %param.11) | copy-start | bytes 28

commit v3 on v2

--- a/solution.py
+++ b/solution.py
@@ -159,70 +159,79 @@
     def pick(first, width):
         total = jnp.zeros((CHUNK, width), F32)
         for j in range(4):
-            cells = pl.ds(pl.multiple_of(j * CELLS + first, HALO), width)
+            cells = pl.ds(pl.multiple_of(j * CELLS + first, PART), width)
             found = jnp.dot(table[...], picker[:, cells], preferred_element_type=F32)
-            code = child[j : j + 1, pl.ds(pl.multiple_of(first, HALO), width)]
+            code = child[j : j + 1, pl.ds(pl.multiple_of(first, PART), width)]
             group = ((code >> 9) & 1) * N_MEM + (code >> 10)
             for g in range(GROUPS):
                 total = total + jnp.where(group == g, found[g * CHUNK : (g + 1) * CHUNK, :], 0.0)
         return (0.25 * total).astype(BF16)
 
-    def far_copy(i):
+    def far_copy(sub, i):
         return remote(
-            coarse_far.at[mem], coarse_far.at[mem], e_send.at[i], e_recv.at[i], mem_at(MEM_STEPS[i]), space
+            coarse_far.at[sub, mem], coarse_far.at[sub, mem], e_send.at[sub, i], e_recv.at[sub, i],
+            mem_at(MEM_STEPS[i]), space,
         )
 
+    partner = mem_at((0, 1))
+
     def rest_copy(i):
-        return remote(
-            coarse_rest.at[mem], coarse_rest.at[mem], c_send.at[i], c_recv.at[i], mem_at(MEM_STEPS[i]), space
-        )
+        owner = mem if i < 4 else partner
+        target = mem_at(((0, 1), (2, 0), (1, 0), (3, 0), (2, 0), (1, 0), (3, 0))[i])
+        return remote(coarse_rest.at[owner], coarse_rest.at[owner], c_send.at[i], c_recv.at[i], target, space)
 
     far = core * (CELLS - HALO)
     near = (1 - core) * (CELLS - HALO)
-    coarse_far[mem] = pick(far, HALO)
-    for i in range(N_MEM - 1):
-        far_copy(i).start()
+    for sub in range(2):
+        coarse_far[sub, mem] = pick(far + sub * PART, PART)
+        for i in range(N_MEM - 1):
+            far_copy(sub, i).start()
     coarse_rest[mem, :, 0:HALO] = pick(near, HALO)
     coarse_rest[mem, :, HALO : 2 * HALO] = pick(HALO, HALO)
     coarse_rest[mem, :, 2 * HALO : 3 * HALO] = pick(2 * HALO, HALO)
-    for i in range(N_MEM - 1):
+    for i in range(4):
         rest_copy(i).start()
 
     two = modes_two[...].astype(BF16)
 
     def reduce_cells(pair, first, coarse):
+        width = coarse.shape[1]
         for i in range(2):
-            pert = ens[2 * pair + i, :, pl.ds(pl.multiple_of(first, HALO), HALO)]
-            prod[i * LEV_PAD : i * LEV_PAD + LEV, :] = pert * coarse
-        value = jnp.dot(two, prod[...], preferred_element_type=F32).astype(BF16)
-        red[pair * ROWS : (pair + 1) * ROWS, pl.ds(pl.multiple_of(HALO + first, HALO), HALO)] = value
-
-    def halo_copy(side, pair):
-        rows = pl.ds(pair * ROWS, ROWS)
-        first, place, target = (
-            (far, (1 - core) * (HALO + CELLS), lax.rem(space + 2 * core + N_SPACE - 1, N_SPACE)),
-            (near, core * (HALO + CELLS), space + 1 - 2 * core),
-        )[side]
+            pert = ens[2 * pair + i, :, pl.ds(pl.multiple_of(first, PART), width)]
+            prod[i * LEV_PAD : i * LEV_PAD + LEV, 0:width] = pert * coarse
+        value = jnp.dot(two, prod[:, 0:width], preferred_element_type=F32).astype(BF16)
+        red[pair * ROWS : (pair + 1) * ROWS, pl.ds(pl.multiple_of(HALO + first, PART), width)] = value
+
+    def halo_copy(n):
+        first, place, target, width = (
+            (far, (1 - core) * (HALO + CELLS), lax.rem(space + 2 * core + N_SPACE - 1, N_SPACE), PART),
+            (far + PART, (1 - core) * (HALO + CELLS) + PART, lax.rem(space + 2 * core + N_SPACE - 1, N_SPACE), PART),
+            (near, core * (HALO + CELLS), space + 1 - 2 * core, HALO),
+        )[n]
         return remote(
-            red.at[rows, pl.ds(pl.multiple_of(HALO + first, HALO), HALO)],
-            red.at[rows, pl.ds(pl.multiple_of(place, HALO), HALO)],
-            h_send.at[side, pair], h_recv.at[side, pair], mem, target,
+            red.at[:, pl.ds(pl.multiple_of(HALO + first, PART), width)],
+            red.at[:, pl.ds(pl.multiple_of(place, PART), width)],
+            h_send.at[n], h_recv.at[n], mem, target,
         )
 
     loads[3].wait()
-    for i in range(N_MEM - 1):
-        far_copy(i).wait()
-    coarse = coarse_far[...].reshape(LEV_PAD, HALO)[0:LEV]
-    for pair in range(PAIRS):
-        reduce_cells(pair, far, coarse)
-        halo_copy(0, pair).start()
-
-    for i in range(N_MEM - 1):
+    for sub in range(2):
+        for i in range(N_MEM - 1):
+            far_copy(sub, i).wait()
+        coarse = coarse_far[sub].reshape(LEV_PAD, PART)[0:LEV]
+        for pair in range(PAIRS):
+            reduce_cells(pair, far + sub * PART, coarse)
+        halo_copy(sub).start()
+
+    rest_copy(0).wait()
+    for i in range(4, N_MEM - 1):
+        rest_copy(i).start()
+    for i in range(1, N_MEM - 1):
         rest_copy(i).wait()
     coarse = coarse_rest[:, :, 0:HALO].reshape(LEV_PAD, HALO)[0:LEV]
     for pair in range(PAIRS):
         reduce_cells(pair, near, coarse)
-        halo_copy(1, pair).start()
+    halo_copy(2).start()
     for half in range(2):
         coarse = coarse_rest[:, :, (half + 1) * HALO : (half + 2) * HALO].reshape(LEV_PAD, HALO)[0:LEV]
         for pair in range(PAIRS):
@@ -235,9 +244,8 @@
         window = red[:, HALO + cells : HALO + cells + SPAN]
         mid_out[:, cells : cells + PART] = jnp.dot(window, weights, preferred_element_type=F32)
 
-    for side in range(2):
-        for pair in range(PAIRS):
-            halo_copy(side, pair).wait()
+    for n in range(3):
+        halo_copy(n).wait()
 
 
 def edge_kernel(halo_rows, ext, stencil, mid, out, result, sems):
@@ -297,7 +305,7 @@
             pltpu.VMEM((N_SPACE, SEND, LEV_PAD), BF16),
             pltpu.VMEM((2 * LEV_PAD, CODES), BF16),
             pltpu.VMEM((CODES, 4 * CELLS), BF16),
-            pltpu.VMEM((N_MEM, CHUNK, HALO), BF16),
+            pltpu.VMEM((2, N_MEM, CHUNK, PART), BF16),
             pltpu.VMEM((N_MEM, CHUNK, 3 * HALO), BF16),
             pltpu.VMEM((2 * LEV_PAD, HALO), BF16),
             pltpu.VMEM((ROWS, 2 * LEV_PAD), F32),
@@ -306,12 +314,12 @@
             dma((2, N_MEM)),
             dma((2, N_SPACE // 2)),
             dma((2, N_SPACE // 2)),
+            dma((2, N_MEM)),
+            dma((2, N_MEM)),
             dma((N_MEM,)),
             dma((N_MEM,)),
-            dma((N_MEM,)),
-            dma((N_MEM,)),
-            dma((2, PAIRS)),
-            dma((2, PAIRS)),
+            dma((3,)),
+            dma((3,)),
         ],
         compiler_params=pltpu.CompilerParams(
             collective_id=0, has_side_effects=True, vmem_limit_bytes=40 * 2**20

time: 43.6 us -> 41.1 us (0.943)
  Pallas kernels: 43.5 us -> 41 us
    pallas_call x1, Pallas kernels: 40.8 us -> 38.3 us  [local(): pl.pallas_call(reduce_kernel, out_shape=(jax.ShapeDtypeStruct((ALL_ROWS,...]
where the time goes in v3:
time: 41.1 us
  Pallas kernels  41 us (100%)
    pallas_call x1, Pallas kernels, local(): pl.pallas_call(reduce_kernel, out_shape=(jax.ShapeDtypeStruct((ALL_ROWS,...  38.3 us
    pallas_call x1, Pallas kernels, local(): pl.pallas_call(edge_kernel, out_shape=jax.ShapeDtypeStruct((ALL_ROWS, CEL...  2.76 us

profile of v3, /device:TPU:1, one launch (start us, length us, event | category | flops | bytes accessed | tf_op | source)
XLA Modules:
  0.0 41.1 jit_solution(6085853781879058233)
XLA Ops:
  0.0 0.0 copy-start
  0.0 0.0 copy-start.1
  0.0 38.3 %reduce.1 = (bf16[400,3072]{1,0:T(8,128)(2,1)S(1)}, f32[400,1024]{1,0:T(8,128)S(1)}) custom-call(f32[127,1024]{1,0:T(8,128)} %grad_hbm.1, s32[4,2048]{1,0:T(4,128)} %child_hbm.1, bf16[40,127]{1,0:T(8,128)(2,1)} %bitcast.4, bf16[10,127,2048]{2,1,0:T(8,128)(2,1)} %ens_hbm.1, bf16[1152,2048]{1,0:T(8,128)(2,1)} %stencil.1), custom_call_target="tpu_custom_call" | custom-call | tf_op jit(solution)/shard_map/reduce/pallas_call | solution.py:288
  38.3 0.0 copy-done
  38.3 0.0 copy-done.1
  38.3 2.8 %edges.1 = f32[400,2048]{1,0:T(8,128)} custom-call(s32[1,2]{1,0:T(1,128)S(1)} %bitcast.3, bf16[400,3072]{1,0:T(8,128)(2,1)S(1)} %get-tuple-element.7.ext, bf16[1152,2048]{1,0:T(8,128)(2,1)S(1)} %copy-done, f32[400,1024]{1,0:T(8,128)S(1)} %get-tuple-element.8.mid), custom_call_target="tpu_custom_call" | custom-call | tf_op jit(solution)/shard_map/edges/pallas_call | solution.py:330
Async XLA Ops:
  0.0 38.3 %copy-start = (bf16[1152,2048]{1,0:T(8,128)(2,1)S(1)}, bf16[1152,2048]{1,0:T(8,128)(2,1)}, u32[]{:S(2)}) copy-start(bf16[1152,2048]{1,0:T(8,128)(2,1)} %stencil.1) | copy-start | bytes 14155780
  0.0 38.3 %copy-start.1 = (s32[2,1]{0,1:T(1,128)S(1)}, s32[2,1]{0,1:T(1,128)}, u32[]{:S(2)}) copy-start(s32[2,1]{0,1:T(1,128)} %param.11) | copy-start | bytes 28

commit v4 on v3

--- a/solution.py
+++ b/solution.py
@@ -27,6 +27,7 @@
 ROWS = 2 * MODES
 ALL_ROWS = PAIRS * ROWS
 MID = CELLS - 2 * HALO
+FAR_SUBS = ((0, 2 * TILE), (2 * TILE, HALO - 2 * TILE))
 PART = 2 * TILE
 SPAN = PART + 2 * HALO
 
@@ -47,18 +48,26 @@
     )
 
 
-def paired(even, odd):
-    blank = jnp.zeros((TILE, TILE), even.dtype)
-    return jnp.concatenate(
-        [jnp.concatenate([even, blank], axis=0), jnp.concatenate([blank, odd], axis=0)], axis=1
-    )
+def paired(stencil, cells, low, high):
+    depth = TILE + 2 * HALO
+    even = [stencil[low : min(high, depth), cells : cells + TILE]]
+    if high > depth:
+        even.append(jnp.zeros((high - depth, TILE), BF16))
+    odd = [stencil[max(low - TILE, 0) : high - TILE, cells + TILE : cells + PART]]
+    if low < TILE:
+        odd.insert(0, jnp.zeros((TILE - low, TILE), BF16))
+    return jnp.concatenate([jnp.concatenate(even, axis=0), jnp.concatenate(odd, axis=0)], axis=1)
+
+
+def own_rows(cells):
+    return max(HALO - cells, 0), min(SPAN, HALO + CELLS - cells)
 
 
 def reduce_kernel(
-    grad_hbm, child_hbm, modes_hbm, ens_hbm, stencil_hbm, red, mid_out,
-    grad, child, modes, ens, stencil, gb, got_levels, turned, got_cols, table, picker,
-    coarse_far, coarse_rest, prod, modes_two,
-    in_sem, m_send, m_recv, s_send, s_recv, e_send, e_recv, c_send, c_recv, h_send, h_recv,
+    grad_hbm, child_hbm, modes_hbm, ens_hbm, stencil_hbm, red, own, stencil,
+    grad, child, modes, ens, gb, got_levels, turned, got_cols, table, picker,
+    coarse_far, coarse_near, coarse_mid, prod, modes_two,
+    in_sem, m_send, m_recv, s_send, s_recv, e_send, e_recv, n_send, n_recv, c_send, c_recv, f_send, f_recv, h_send, h_recv,
 ):
     mem = lax.axis_index("mem")
     space = lax.axis_index("space")
@@ -79,12 +88,11 @@
                 (modes_hbm, modes),
                 (child_hbm, child),
                 (ens_hbm, ens),
-                (stencil_hbm.at[:, pl.ds(HALO, MID)], stencil),
+                (stencil_hbm, stencil),
             )
         )
     ]
-    for load in loads:
-        load.start()
+    loads[0].start()
 
     barrier = pltpu.get_barrier_semaphore()
     for step in OTHER_STEPS:
@@ -114,6 +122,8 @@
     for k in range(2):
         for i in range(N_MEM - 1):
             level_copy(k, i).start()
+    for load in loads[1:]:
+        load.start()
 
     got_levels[mem] = gb[mem]
 
@@ -159,116 +169,143 @@
     def pick(first, width):
         total = jnp.zeros((CHUNK, width), F32)
         for j in range(4):
-            cells = pl.ds(pl.multiple_of(j * CELLS + first, PART), width)
+            cells = pl.ds(pl.multiple_of(j * CELLS + first, TILE), width)
             found = jnp.dot(table[...], picker[:, cells], preferred_element_type=F32)
-            code = child[j : j + 1, pl.ds(pl.multiple_of(first, PART), width)]
+            code = child[j : j + 1, pl.ds(pl.multiple_of(first, TILE), width)]
             group = ((code >> 9) & 1) * N_MEM + (code >> 10)
             for g in range(GROUPS):
                 total = total + jnp.where(group == g, found[g * CHUNK : (g + 1) * CHUNK, :], 0.0)
         return (0.25 * total).astype(BF16)
 
     def far_copy(sub, i):
-        return remote(
-            coarse_far.at[sub, mem], coarse_far.at[sub, mem], e_send.at[sub, i], e_recv.at[sub, i],
+        cols = pl.ds(*FAR_SUBS[sub])
+        return remote(
+            coarse_far.at[mem, :, cols], coarse_far.at[mem, :, cols], e_send.at[sub, i], e_recv.at[sub, i],
             mem_at(MEM_STEPS[i]), space,
         )
 
+    def near_copy(i):
+        return remote(
+            coarse_near.at[mem], coarse_near.at[mem], n_send.at[i], n_recv.at[i], mem_at(MEM_STEPS[i]), space
+        )
+
     partner = mem_at((0, 1))
 
-    def rest_copy(i):
+    def mid_copy(half, i):
         owner = mem if i < 4 else partner
         target = mem_at(((0, 1), (2, 0), (1, 0), (3, 0), (2, 0), (1, 0), (3, 0))[i])
-        return remote(coarse_rest.at[owner], coarse_rest.at[owner], c_send.at[i], c_recv.at[i], target, space)
+        return remote(
+            coarse_mid.at[half, owner], coarse_mid.at[half, owner], c_send.at[half, i], c_recv.at[half, i], target, space
+        )
 
     far = core * (CELLS - HALO)
     near = (1 - core) * (CELLS - HALO)
-    for sub in range(2):
-        coarse_far[sub, mem] = pick(far + sub * PART, PART)
+    for sub, (cells, width) in enumerate(FAR_SUBS):
+        coarse_far[mem, :, cells : cells + width] = pick(far + cells, width)
         for i in range(N_MEM - 1):
             far_copy(sub, i).start()
-    coarse_rest[mem, :, 0:HALO] = pick(near, HALO)
-    coarse_rest[mem, :, HALO : 2 * HALO] = pick(HALO, HALO)
-    coarse_rest[mem, :, 2 * HALO : 3 * HALO] = pick(2 * HALO, HALO)
-    for i in range(4):
-        rest_copy(i).start()
+    for half in range(2):
+        coarse_mid[half, mem] = pick(HALO * (half + 1), HALO)
+        for i in range(4):
+            mid_copy(half, i).start()
+    coarse_near[mem] = pick(near, HALO)
+    for i in range(N_MEM - 1):
+        near_copy(i).start()
 
     two = modes_two[...].astype(BF16)
 
     def reduce_cells(pair, first, coarse):
         width = coarse.shape[1]
         for i in range(2):
-            pert = ens[2 * pair + i, :, pl.ds(pl.multiple_of(first, PART), width)]
+            pert = ens[2 * pair + i, :, pl.ds(pl.multiple_of(first, TILE), width)]
             prod[i * LEV_PAD : i * LEV_PAD + LEV, 0:width] = pert * coarse
         value = jnp.dot(two, prod[:, 0:width], preferred_element_type=F32).astype(BF16)
-        red[pair * ROWS : (pair + 1) * ROWS, pl.ds(pl.multiple_of(HALO + first, PART), width)] = value
-
-    def halo_copy(n):
-        first, place, target, width = (
-            (far, (1 - core) * (HALO + CELLS), lax.rem(space + 2 * core + N_SPACE - 1, N_SPACE), PART),
-            (far + PART, (1 - core) * (HALO + CELLS) + PART, lax.rem(space + 2 * core + N_SPACE - 1, N_SPACE), PART),
-            (near, core * (HALO + CELLS), space + 1 - 2 * core, HALO),
-        )[n]
-        return remote(
-            red.at[:, pl.ds(pl.multiple_of(HALO + first, PART), width)],
-            red.at[:, pl.ds(pl.multiple_of(place, PART), width)],
-            h_send.at[n], h_recv.at[n], mem, target,
+        red[pair * ROWS : (pair + 1) * ROWS, pl.ds(pl.multiple_of(HALO + first, TILE), width)] = value
+
+    far_target = lax.rem(space + 2 * core + N_SPACE - 1, N_SPACE)
+    far_place = (1 - core) * (HALO + CELLS)
+
+    def far_halo(sub):
+        cells, width = FAR_SUBS[sub]
+        return remote(
+            red.at[:, pl.ds(pl.multiple_of(HALO + far + cells, TILE), width)],
+            red.at[:, pl.ds(pl.multiple_of(far_place + cells, TILE), width)],
+            f_send.at[sub], f_recv.at[sub], mem, far_target,
+        )
+
+    def near_halo(pair):
+        rows = pl.ds(pair * ROWS, ROWS)
+        return remote(
+            red.at[rows, pl.ds(pl.multiple_of(HALO + near, HALO), HALO)],
+            red.at[rows, pl.ds(pl.multiple_of(core * (HALO + CELLS), HALO), HALO)],
+            h_send.at[pair], h_recv.at[pair], mem, space + 1 - 2 * core,
         )
 
     loads[3].wait()
-    for sub in range(2):
+    for sub, (cells, width) in enumerate(FAR_SUBS):
         for i in range(N_MEM - 1):
             far_copy(sub, i).wait()
-        coarse = coarse_far[sub].reshape(LEV_PAD, PART)[0:LEV]
+        coarse = coarse_far[:, :, cells : cells + width].reshape(LEV_PAD, width)[0:LEV]
         for pair in range(PAIRS):
-            reduce_cells(pair, far + sub * PART, coarse)
-        halo_copy(sub).start()
-
-    rest_copy(0).wait()
-    for i in range(4, N_MEM - 1):
-        rest_copy(i).start()
-    for i in range(1, N_MEM - 1):
-        rest_copy(i).wait()
-    coarse = coarse_rest[:, :, 0:HALO].reshape(LEV_PAD, HALO)[0:LEV]
+            reduce_cells(pair, far + cells, coarse)
+        far_halo(sub).start()
+
+    for half in range(2):
+        mid_copy(half, 0).wait()
+        for i in range(4, N_MEM - 1):
+            mid_copy(half, i).start()
+
+    for i in range(N_MEM - 1):
+        near_copy(i).wait()
+    coarse = coarse_near[...].reshape(LEV_PAD, HALO)[0:LEV]
     for pair in range(PAIRS):
         reduce_cells(pair, near, coarse)
-    halo_copy(2).start()
+        near_halo(pair).start()
+
+    loads[4].wait()
+    done = 0
     for half in range(2):
-        coarse = coarse_rest[:, :, (half + 1) * HALO : (half + 2) * HALO].reshape(LEV_PAD, HALO)[0:LEV]
+        for i in range(1, N_MEM - 1):
+            mid_copy(half, i).wait()
+        coarse = coarse_mid[half].reshape(LEV_PAD, HALO)[0:LEV]
         for pair in range(PAIRS):
             reduce_cells(pair, HALO * (half + 1), coarse)
-
-    loads[4].wait()
-    for part in range(MID // PART):
-        cells = part * PART
-        weights = paired(stencil[:, cells : cells + TILE], stencil[:, cells + TILE : cells + PART])
-        window = red[:, HALO + cells : HALO + cells + SPAN]
-        mid_out[:, cells : cells + PART] = jnp.dot(window, weights, preferred_element_type=F32)
-
-    for n in range(3):
-        halo_copy(n).wait()
-
-
-def edge_kernel(halo_rows, ext, stencil, mid, out, result, sems):
-    mid_copy = pltpu.make_async_copy(mid, out.at[:, pl.ds(HALO, MID)], sems.at[0])
+        for part in range(done, (2, CELLS // PART)[half]):
+            cells = part * PART
+            low, high = own_rows(cells)
+            own[:, cells : cells + PART] = jnp.dot(
+                red[:, cells + low : cells + high], paired(stencil, cells, low, high), preferred_element_type=F32
+            )
+        done = 2
+
+    for pair in range(PAIRS):
+        near_halo(pair).wait()
+    for sub in range(2):
+        far_halo(sub).wait()
+
+
+def edge_kernel(halo_rows, ext, own, stencil, out, result, sems):
+    mid_copy = pltpu.make_async_copy(own.at[:, pl.ds(HALO, MID)], out.at[:, pl.ds(HALO, MID)], sems.at[0])
     mid_copy.start()
     copies = [mid_copy]
 
     col = lax.broadcasted_iota(jnp.int32, (16, HALO), 1)
     low_kept = (col >= HALO - halo_rows[0, 0]).astype(F32).astype(BF16)[0:1]
     high_kept = (col < halo_rows[0, 1]).astype(F32).astype(BF16)[0:1]
-    low = ext[:, 0:HALO] * low_kept
-    high = ext[:, HALO + CELLS : EXT] * high_kept
 
     for n, part in enumerate((0, 1, CELLS // PART - 2, CELLS // PART - 1)):
         cells = part * PART
+        low, high = own_rows(cells)
         if part < 2:
-            window = jnp.concatenate([low[:, cells:], ext[:, HALO : cells + SPAN]], axis=1)
+            low, high = 0, low
+            kept = low_kept[:, cells:]
         else:
-            window = jnp.concatenate(
-                [ext[:, cells : HALO + CELLS], high[:, 0 : cells + SPAN - HALO - CELLS]], axis=1
-            )
-        weights = paired(stencil[:, cells : cells + TILE], stencil[:, cells + TILE : cells + PART])
-        result[n] = jnp.dot(window, weights, preferred_element_type=F32)
+            low, high = high, SPAN
+            kept = high_kept[:, 0 : high - low]
+        window = ext[:, cells + low : cells + high] * kept
+        result[n] = own[:, cells : cells + PART] + jnp.dot(
+            window, paired(stencil, cells, low, high), preferred_element_type=F32
+        )
         copy = pltpu.make_async_copy(result.at[n], out.at[:, pl.ds(cells, PART)], sems.at[n + 1])
         copy.start()
         copies.append(copy)
@@ -285,28 +322,29 @@
         pltpu.with_memory_space_constraint(x, pltpu.HBM)
         for x in (grad_hi, child_map, vert_modes.T, ens_pert, loc_stencil)
     ]
-    ext, mid = pl.pallas_call(
+    ext, own, stencil = pl.pallas_call(
         reduce_kernel,
         out_shape=(
             jax.ShapeDtypeStruct((ALL_ROWS, EXT), BF16),
-            jax.ShapeDtypeStruct((ALL_ROWS, MID), F32),
+            jax.ShapeDtypeStruct((ALL_ROWS, CELLS), F32),
+            jax.ShapeDtypeStruct((TILE + 2 * HALO, CELLS), BF16),
         ),
         in_specs=[hbm] * 5,
-        out_specs=(vmem, vmem),
+        out_specs=(vmem, vmem, vmem),
         scratch_shapes=[
             pltpu.VMEM((LEV, HI), F32),
             pltpu.VMEM((4, CELLS), jnp.int32),
             pltpu.VMEM((MODES, LEV), BF16),
             pltpu.VMEM((2 * PAIRS, LEV, CELLS), BF16),
-            pltpu.VMEM((TILE + 2 * HALO, MID), BF16),
             pltpu.VMEM((N_MEM, CHUNK, HI), BF16),
             pltpu.VMEM((N_MEM, CHUNK, HI), BF16),
             pltpu.VMEM((N_SPACE, SEND, LEV_PAD), BF16),
             pltpu.VMEM((N_SPACE, SEND, LEV_PAD), BF16),
             pltpu.VMEM((2 * LEV_PAD, CODES), BF16),
             pltpu.VMEM((CODES, 4 * CELLS), BF16),
-            pltpu.VMEM((2, N_MEM, CHUNK, PART), BF16),
-            pltpu.VMEM((N_MEM, CHUNK, 3 * HALO), BF16),
+            pltpu.VMEM((N_MEM, CHUNK, HALO), BF16),
+            pltpu.VMEM((N_MEM, CHUNK, HALO), BF16),
+            pltpu.VMEM((2, N_MEM, CHUNK, HALO), BF16),
             pltpu.VMEM((2 * LEV_PAD, HALO), BF16),
             pltpu.VMEM((ROWS, 2 * LEV_PAD), F32),
             dma((5,)),
@@ -318,8 +356,12 @@
             dma((2, N_MEM)),
             dma((N_MEM,)),
             dma((N_MEM,)),
-            dma((3,)),
-            dma((3,)),
+            dma((2, N_MEM)),
+            dma((2, N_MEM)),
+            dma((2,)),
+            dma((2,)),
+            dma((PAIRS,)),
+            dma((PAIRS,)),
         ],
         compiler_params=pltpu.CompilerParams(
             collective_id=0, has_side_effects=True, vmem_limit_bytes=40 * 2**20
@@ -330,12 +372,12 @@
     out = pl.pallas_call(
         edge_kernel,
         out_shape=jax.ShapeDtypeStruct((ALL_ROWS, CELLS), F32),
-        in_specs=[pl.BlockSpec(memory_space=pltpu.SMEM), vmem, vmem, anywhere],
+        in_specs=[pl.BlockSpec(memory_space=pltpu.SMEM), vmem, vmem, vmem],
         out_specs=anywhere,
         scratch_shapes=[pltpu.VMEM((4, ALL_ROWS, PART), F32), dma((5,))],
         compiler_params=pltpu.CompilerParams(vmem_limit_bytes=40 * 2**20),
         name="edges",
-    )(halo_rows.T, ext, loc_stencil, mid)
+    )(halo_rows.T, ext, own, stencil)
     return out.reshape(2 * PAIRS, MODES, CELLS)
 
 

time: 41.1 us -> 40.2 us (0.978)
  Pallas kernels: 41 us -> 40 us
    pallas_call x1, Pallas kernels: 38.3 us -> 37.7 us  [local(): pl.pallas_call(reduce_kernel, out_shape=(jax.ShapeDtypeStruct((ALL_ROWS,...]
where the time goes in v4:
time: 40.2 us; the launch traced here: 40.1 us
  Pallas kernels  40 us (100%)
    pallas_call x1, Pallas kernels, local(): pl.pallas_call(reduce_kernel, out_shape=(jax.ShapeDtypeStruct((ALL_ROWS,...  37.7 us
    pallas_call x1, Pallas kernels, local(): pl.pallas_call(edge_kernel, out_shape=jax.ShapeDtypeStruct((ALL_ROWS, CEL...  2.36 us

profile of v4, /device:TPU:1, one launch (start us, length us, event | category | flops | bytes accessed | tf_op | source)
XLA Modules:
  0.0 40.1 jit_solution(2116219392005697917)
XLA Ops:
  0.0 0.0 copy-start
  0.0 37.7 %reduce.1 = (bf16[400,3072]{1,0:T(8,128)(2,1)S(1)}, f32[400,2048]{1,0:T(8,128)S(1)}, bf16[1152,2048]{1,0:T(8,128)(2,1)S(1)}) custom-call(f32[127,1024]{1,0:T(8,128)} %grad_hbm.1, s32[4,2048]{1,0:T(4,128)} %child_hbm.1, bf16[40,127]{1,0:T(8,128)(2,1)} %bitcast.4, bf16[10,127,2048]{2,1,0:T(8,128)(2,1)} %ens_hbm.1, bf16[1152,2048]{1,0:T(8,128)(2,1)} %stencil_hbm.1), custom_call_target="tpu_custom_call" | custom-call | tf_op jit(solution)/shard_map/reduce/pallas_call | solution.py:325
  37.7 0.0 copy-done
  37.7 2.4 %edges.1 = f32[400,2048]{1,0:T(8,128)} custom-call(s32[1,2]{1,0:T(1,128)S(1)} %bitcast.3, bf16[400,3072]{1,0:T(8,128)(2,1)S(1)} %get-tuple-element.8.ext, f32[400,2048]{1,0:T(8,128)S(1)} %get-tuple-element.9.own, bf16[1152,2048]{1,0:T(8,128)(2,1)S(1)} %get-tuple-element.10.stencil), custom_call_target="tpu_custom_call" | custom-call | tf_op jit(solution)/shard_map/edges/pallas_call | solution.py:372
Async XLA Ops:
  0.0 37.7 %copy-start = (s32[2,1]{0,1:T(1,128)S(1)}, s32[2,1]{0,1:T(1,128)}, u32[]{:S(2)}) copy-start(s32[2,1]{0,1:T(1,128)} %param.11) | copy-start | bytes 28

commit v5 on v4

--- a/solution.py
+++ b/solution.py
@@ -110,7 +110,7 @@
 
     pl.semaphore_wait(barrier, N_MEM - 1 + N_SPACE - 1)
 
-    sides = (x_lo, 1 - x_lo)
+    sides = (1 - x_lo, x_lo)
 
     def level_copy(k, i):
         target = mem_at(MEM_STEPS[i])
@@ -135,10 +135,10 @@
     prod[...] = jnp.zeros_like(prod)
 
     def column_copy(k, i):
-        target = space_at(sides[k], (OWN_STEPS, OTHER_STEPS)[k][i])
+        target = space_at(sides[k], (OTHER_STEPS, OWN_STEPS)[k][i])
         return remote(turned.at[target], got_cols.at[space], s_send.at[k, i], s_recv.at[k, i], mem, target)
 
-    counts = (len(OWN_STEPS), len(OTHER_STEPS))
+    counts = (len(OTHER_STEPS), len(OWN_STEPS))
     for k in range(2):
         for i in range(N_MEM - 1):
             level_copy(k, i).wait()
@@ -218,8 +218,8 @@
         width = coarse.shape[1]
         for i in range(2):
             pert = ens[2 * pair + i, :, pl.ds(pl.multiple_of(first, TILE), width)]
-            prod[i * LEV_PAD : i * LEV_PAD + LEV, 0:width] = pert * coarse
-        value = jnp.dot(two, prod[:, 0:width], preferred_element_type=F32).astype(BF16)
+            prod[pair, i * LEV_PAD : i * LEV_PAD + LEV, 0:width] = pert * coarse
+        value = jnp.dot(two, prod[pair, :, 0:width], preferred_element_type=F32).astype(BF16)
         red[pair * ROWS : (pair + 1) * ROWS, pl.ds(pl.multiple_of(HALO + first, TILE), width)] = value
 
     far_target = lax.rem(space + 2 * core + N_SPACE - 1, N_SPACE)
@@ -345,7 +345,7 @@
             pltpu.VMEM((N_MEM, CHUNK, HALO), BF16),
             pltpu.VMEM((N_MEM, CHUNK, HALO), BF16),
             pltpu.VMEM((2, N_MEM, CHUNK, HALO), BF16),
-            pltpu.VMEM((2 * LEV_PAD, HALO), BF16),
+            pltpu.VMEM((PAIRS, 2 * LEV_PAD, HALO), BF16),
             pltpu.VMEM((ROWS, 2 * LEV_PAD), F32),
             dma((5,)),
             dma((2, N_MEM)),

time: 40.2 us -> 39.6 us (0.985)
  Pallas kernels: 40 us -> 39.4 us
    pallas_call x1, Pallas kernels: 37.7 us -> 37 us  [local(): pl.pallas_call(reduce_kernel, out_shape=(jax.ShapeDtypeStruct((ALL_ROWS,...]
where the time goes in v5:
time: 39.6 us; the launch traced here: 39.4 us
  Pallas kernels  39.4 us (99%)
    pallas_call x1, Pallas kernels, local(): pl.pallas_call(reduce_kernel, out_shape=(jax.ShapeDtypeStruct((ALL_ROWS,...  37 us
    pallas_call x1, Pallas kernels, local(): pl.pallas_call(edge_kernel, out_shape=jax.ShapeDtypeStruct((ALL_ROWS, CEL...  2.36 us

profile of v5, /device:TPU:1, one launch (start us, length us, event | category | flops | bytes accessed | tf_op | source)
XLA Modules:
  0.0 39.4 jit_solution(5265439318474452336)
XLA Ops:
  0.0 0.0 copy-start
  0.0 37.0 %reduce.1 = (bf16[400,3072]{1,0:T(8,128)(2,1)S(1)}, f32[400,2048]{1,0:T(8,128)S(1)}, bf16[1152,2048]{1,0:T(8,128)(2,1)S(1)}) custom-call(f32[127,1024]{1,0:T(8,128)} %grad_hbm.1, s32[4,2048]{1,0:T(4,128)} %child_hbm.1, bf16[40,127]{1,0:T(8,128)(2,1)} %bitcast.4, bf16[10,127,2048]{2,1,0:T(8,128)(2,1)} %ens_hbm.1, bf16[1152,2048]{1,0:T(8,128)(2,1)} %stencil_hbm.1), custom_call_target="tpu_custom_call" | custom-call | tf_op jit(solution)/shard_map/reduce/pallas_call | solution.py:325
  37.0 0.0 copy-done
  37.1 2.4 %edges.1 = f32[400,2048]{1,0:T(8,128)} custom-call(s32[1,2]{1,0:T(1,128)S(1)} %bitcast.3, bf16[400,3072]{1,0:T(8,128)(2,1)S(1)} %get-tuple-element.8.ext, f32[400,2048]{1,0:T(8,128)S(1)} %get-tuple-element.9.own, bf16[1152,2048]{1,0:T(8,128)(2,1)S(1)} %get-tuple-element.10.stencil), custom_call_target="tpu_custom_call" | custom-call | tf_op jit(solution)/shard_map/edges/pallas_call | solution.py:372
Async XLA Ops:
  0.0 37.0 %copy-start = (s32[2,1]{0,1:T(1,128)S(1)}, s32[2,1]{0,1:T(1,128)}, u32[]{:S(2)}) copy-start(s32[2,1]{0,1:T(1,128)} %param.11) | copy-start | bytes 28

commit v6 on v5

--- a/solution.py
+++ b/solution.py
@@ -141,7 +141,7 @@
     counts = (len(OTHER_STEPS), len(OWN_STEPS))
     for k in range(2):
         for i in range(N_MEM - 1):
-            level_copy(k, i).wait()
+            level_copy(k, i).wait_recv()
         for q in range(CODES // 128):
             first = pl.multiple_of(sides[k] * CODES + q * 128, 128)
             part = got_levels[:, :, pl.ds(first, 128)].reshape(LEV_PAD, 128)
@@ -162,7 +162,7 @@
 
     for k in range(2):
         for i in range(counts[k]):
-            column_copy(k, i).wait()
+            column_copy(k, i).wait_recv()
         cols = got_cols[pl.ds(sides[k] * 16, 16)].reshape(CODES, LEV_PAD)
         table[pl.ds(pl.multiple_of(sides[k] * LEV_PAD, LEV_PAD), LEV_PAD), :] = cols.T
 
@@ -244,19 +244,19 @@
     loads[3].wait()
     for sub, (cells, width) in enumerate(FAR_SUBS):
         for i in range(N_MEM - 1):
-            far_copy(sub, i).wait()
+            far_copy(sub, i).wait_recv()
         coarse = coarse_far[:, :, cells : cells + width].reshape(LEV_PAD, width)[0:LEV]
         for pair in range(PAIRS):
             reduce_cells(pair, far + cells, coarse)
         far_halo(sub).start()
 
     for half in range(2):
-        mid_copy(half, 0).wait()
+        mid_copy(half, 0).wait_recv()
         for i in range(4, N_MEM - 1):
             mid_copy(half, i).start()
 
     for i in range(N_MEM - 1):
-        near_copy(i).wait()
+        near_copy(i).wait_recv()
     coarse = coarse_near[...].reshape(LEV_PAD, HALO)[0:LEV]
     for pair in range(PAIRS):
         reduce_cells(pair, near, coarse)
@@ -266,7 +266,7 @@
     done = 0
     for half in range(2):
         for i in range(1, N_MEM - 1):
-            mid_copy(half, i).wait()
+            mid_copy(half, i).wait_recv()
         coarse = coarse_mid[half].reshape(LEV_PAD, HALO)[0:LEV]
         for pair in range(PAIRS):
             reduce_cells(pair, HALO * (half + 1), coarse)
@@ -278,6 +278,16 @@
             )
         done = 2
 
+    for k in range(2):
+        for i in range(N_MEM - 1):
+            level_copy(k, i).wait_send()
+        for i in range(counts[k]):
+            column_copy(k, i).wait_send()
+    for i in range(N_MEM - 1):
+        for n in range(2):
+            far_copy(n, i).wait_send()
+            mid_copy(n, i).wait_send()
+        near_copy(i).wait_send()
     for pair in range(PAIRS):
         near_halo(pair).wait()
     for sub in range(2):

time: 39.6 us -> 39.5 us (level)
  no operation moved by 1% of the time
where the time goes in v6:
time: 39.5 us; the launch traced here: 39.4 us
  Pallas kernels  39.3 us (99%)
    pallas_call x1, Pallas kernels, local(): pl.pallas_call(reduce_kernel, out_shape=(jax.ShapeDtypeStruct((ALL_ROWS,...  37 us
    pallas_call x1, Pallas kernels, local(): pl.pallas_call(edge_kernel, out_shape=jax.ShapeDtypeStruct((ALL_ROWS, CEL...  2.36 us

profile of v6, /device:TPU:1, one launch (start us, length us, event | category | flops | bytes accessed | tf_op | source)
XLA Modules:
  0.0 39.4 jit_solution(4585186994973205741)
XLA Ops:
  0.0 0.0 copy-start
  0.0 37.0 %reduce.1 = (bf16[400,3072]{1,0:T(8,128)(2,1)S(1)}, f32[400,2048]{1,0:T(8,128)S(1)}, bf16[1152,2048]{1,0:T(8,128)(2,1)S(1)}) custom-call(f32[127,1024]{1,0:T(8,128)} %grad_hbm.1, s32[4,2048]{1,0:T(4,128)} %child_hbm.1, bf16[40,127]{1,0:T(8,128)(2,1)} %bitcast.4, bf16[10,127,2048]{2,1,0:T(8,128)(2,1)} %ens_hbm.1, bf16[1152,2048]{1,0:T(8,128)(2,1)} %stencil_hbm.1), custom_call_target="tpu_custom_call" | custom-call | tf_op jit(solution)/shard_map/reduce/pallas_call | solution.py:335
  37.0 0.0 copy-done
  37.0 2.4 %edges.1 = f32[400,2048]{1,0:T(8,128)} custom-call(s32[1,2]{1,0:T(1,128)S(1)} %bitcast.3, bf16[400,3072]{1,0:T(8,128)(2,1)S(1)} %get-tuple-element.8.ext, f32[400,2048]{1,0:T(8,128)S(1)} %get-tuple-element.9.own, bf16[1152,2048]{1,0:T(8,128)(2,1)S(1)} %get-tuple-element.10.stencil), custom_call_target="tpu_custom_call" | custom-call | tf_op jit(solution)/shard_map/edges/pallas_call | solution.py:382
Async XLA Ops:
  0.0 37.0 %copy-start = (s32[2,1]{0,1:T(1,128)S(1)}, s32[2,1]{0,1:T(1,128)}, u32[]{:S(2)}) copy-start(s32[2,1]{0,1:T(1,128)} %param.11) | copy-start | bytes 28

commit v7 on v6

--- a/solution.py
+++ b/solution.py
@@ -179,9 +179,18 @@
 
     def far_copy(sub, i):
         cols = pl.ds(*FAR_SUBS[sub])
-        return remote(
-            coarse_far.at[mem, :, cols], coarse_far.at[mem, :, cols], e_send.at[sub, i], e_recv.at[sub, i],
-            mem_at(MEM_STEPS[i]), space,
+        target = i + (mem <= i).astype(jnp.int32)
+        return remote(
+            coarse_far.at[mem, :, cols], coarse_far.at[mem, :, cols], e_send.at[sub, i], e_recv.at[sub, mem],
+            target, space,
+        )
+
+    def far_arrived(sub, d):
+        cols = pl.ds(*FAR_SUBS[sub])
+        source = lax.rem(mem + d, N_MEM)
+        return remote(
+            coarse_far.at[source, :, cols], coarse_far.at[source, :, cols], e_send.at[sub, 0], e_recv.at[sub, source],
+            source, space,
         )
 
     def near_copy(i):
@@ -244,7 +253,7 @@
     loads[3].wait()
     for sub, (cells, width) in enumerate(FAR_SUBS):
         for i in range(N_MEM - 1):
-            far_copy(sub, i).wait_recv()
+            far_arrived(sub, i + 1).wait_recv()
         coarse = coarse_far[:, :, cells : cells + width].reshape(LEV_PAD, width)[0:LEV]
         for pair in range(PAIRS):
             reduce_cells(pair, far + cells, coarse)

time: 39.5 us -> 39.5 us (level)
  no operation moved by 1% of the time
where the time goes in v7:
time: 39.5 us; the launch traced here: 39.4 us
  Pallas kernels  39.3 us (99%)
    pallas_call x1, Pallas kernels, local(): pl.pallas_call(reduce_kernel, out_shape=(jax.ShapeDtypeStruct((ALL_ROWS,...  37 us
    pallas_call x1, Pallas kernels, local(): pl.pallas_call(edge_kernel, out_shape=jax.ShapeDtypeStruct((ALL_ROWS, CEL...  2.36 us

profile of v7, /device:TPU:1, one launch (start us, length us, event | category | flops | bytes accessed | tf_op | source)
XLA Modules:
  0.0 39.4 jit_solution(17884808402883572517)
XLA Ops:
  0.0 0.0 copy-start
  0.0 37.0 %reduce.1 = (bf16[400,3072]{1,0:T(8,128)(2,1)S(1)}, f32[400,2048]{1,0:T(8,128)S(1)}, bf16[1152,2048]{1,0:T(8,128)(2,1)S(1)}) custom-call(f32[127,1024]{1,0:T(8,128)} %grad_hbm.1, s32[4,2048]{1,0:T(4,128)} %child_hbm.1, bf16[40,127]{1,0:T(8,128)(2,1)} %bitcast.4, bf16[10,127,2048]{2,1,0:T(8,128)(2,1)} %ens_hbm.1, bf16[1152,2048]{1,0:T(8,128)(2,1)} %stencil_hbm.1), custom_call_target="tpu_custom_call" | custom-call | tf_op jit(solution)/shard_map/reduce/pallas_call | solution.py:344
  37.0 0.0 copy-done
  37.0 2.4 %edges.1 = f32[400,2048]{1,0:T(8,128)} custom-call(s32[1,2]{1,0:T(1,128)S(1)} %bitcast.3, bf16[400,3072]{1,0:T(8,128)(2,1)S(1)} %get-tuple-element.8.ext, f32[400,2048]{1,0:T(8,128)S(1)} %get-tuple-element.9.own, bf16[1152,2048]{1,0:T(8,128)(2,1)S(1)} %get-tuple-element.10.stencil), custom_call_target="tpu_custom_call" | custom-call | tf_op jit(solution)/shard_map/edges/pallas_call | solution.py:391
Async XLA Ops:
  0.0 37.0 %copy-start = (s32[2,1]{0,1:T(1,128)S(1)}, s32[2,1]{0,1:T(1,128)}, u32[]{:S(2)}) copy-start(s32[2,1]{0,1:T(1,128)} %param.11) | copy-start | bytes 28
